TPU v7x, 32 devices: a whole 2x2x4 slice. The times are simulated.
32 devices in a mesh: rt: 8 (over z, y), mob: 4 (over x, core).
Axes of the slice: x: 2, y: 2, z: 4, core: 2. Of those that a mesh axis runs over, the one named last changes fastest.
Arguments:
- observed: float32 [256, 64, 1280], P('rt', 'mob'), as said below
- frame_kernel: float32 [31], replicated, may hold values from 0.05 to 1
- scan_kernel: float32 [15], replicated, may hold values from 0.05 to 1
- prec_window: int32 [256], P('rt'), may hold values from 0 to 15
- frag_window: int32 [1024], P('mob'), may hold values from 0 to 15
Outputs:
- estimate: float32 [256, 64, 1280], P('rt', 'mob')
- correlation: float32 [256, 1024], P('rt', 'mob')
Inputs may be any that keep to these rules, and one draw needn't show every extreme that they name: `observed`: positive intensities.
All inputs are finite; a program needn't handle non-finite values.
Results may differ from a plain program's by a relative error of at most 0.0003.
Values sent between devices are 32-bit elements; how exact they have to be, the bound alone decides.
A program may use at most 64 MiB of HBM per device.

v0:
```python
import jax
import jax.numpy as jnp
from jax import lax
from jax.sharding import PartitionSpec as P

PREC = 256
ITERS = 2


def extended(cells, sides, width):
    for axis, dim in sides:
        count = lax.axis_size(axis)
        ends = count - 1
        head = lax.slice_in_dim(cells, 0, width, axis=dim)
        tail = lax.slice_in_dim(cells, cells.shape[dim] - width, cells.shape[dim], axis=dim)
        cells = jnp.concatenate(
            [
                lax.ppermute(tail, axis, [(i, (i + 1) % count) for i in range(ends)]),
                cells,
                lax.ppermute(head, axis, [((i + 1) % count, i) for i in range(ends)]),
            ],
            axis=dim,
        )
    return cells


def apply_taps(padded, kernel, along, length):
    running = kernel[0] * lax.slice_in_dim(padded, 0, length, axis=along)
    for tap_index in range(1, kernel.shape[0]):
        running = running + kernel[tap_index] * lax.slice_in_dim(
            padded, tap_index, tap_index + length, axis=along
        )
    return running


def local(observed, frame_kernel, scan_kernel, prec_window, frag_window):
    frames, scan_count, channels = observed.shape
    frame_radius = (frame_kernel.shape[0] - 1) // 2
    scan_radius = (scan_kernel.shape[0] - 1) // 2
    flip_frames = frame_kernel[::-1]
    flip_scans = scan_kernel[::-1]
    estimate = observed
    for iteration in range(ITERS):
        padded_scans = extended(estimate, (("mob", 1),), scan_radius)
        scan_blurred = apply_taps(padded_scans, scan_kernel, 1, scan_count)
        padded_frames = extended(scan_blurred, (("rt", 0),), frame_radius)
        blurred_image = apply_taps(padded_frames, frame_kernel, 0, frames)
        ratio_field = observed / blurred_image
        ratio_frames = extended(ratio_field, (("rt", 0),), frame_radius)
        scan_padded_scans = extended(
            apply_taps(ratio_frames, flip_frames, 0, frames), (("mob", 1),), scan_radius
        )
        estimate = estimate * apply_taps(scan_padded_scans, flip_scans, 1, scan_count)
    profiles = estimate.reshape(frames * scan_count, channels)
    cell_count = frames * scan_count * lax.axis_size("rt") * lax.axis_size("mob")
    channel_total = lax.psum(jnp.sum(profiles, axis=0), ("rt", "mob"))
    channel_mean = channel_total / cell_count
    centered = (profiles - channel_mean).astype(jnp.bfloat16)
    as_float = centered.astype(jnp.float32)
    squares = lax.psum(jnp.sum(as_float * as_float, axis=0), ("rt", "mob"))
    cross_sums = lax.dot_general(
        centered[:, :PREC],
        centered[:, PREC:],
        (((0,), (0,)), ((), ())),
        preferred_element_type=jnp.float32,
    )
    partial_value = lax.psum_scatter(cross_sums, "mob", scatter_dimension=1, tiled=True)
    block_sums = lax.psum_scatter(partial_value, "rt", scatter_dimension=0, tiled=True)
    row_count = prec_window.shape[0]
    column_count = frag_window.shape[0]
    inverse_norm = 1.0 / jnp.sqrt(squares + 1e-06)
    row_inverse = lax.dynamic_slice_in_dim(
        inverse_norm[:PREC], lax.axis_index("rt") * row_count, row_count
    )
    column_inverse = lax.dynamic_slice_in_dim(
        inverse_norm[PREC:], lax.axis_index("mob") * column_count, column_count
    )
    pair_mask = (prec_window[:, None] == frag_window[None, :]).astype(jnp.float32)
    correlation = pair_mask * block_sums * row_inverse[:, None] * column_inverse[None, :]
    return (estimate, correlation)


def solution(mesh):
    placed = (P("rt", "mob", None), P(), P(), P("rt"), P("mob"))
    return jax.shard_map(
        local,
        mesh=mesh,
        in_specs=placed,
        out_specs=(P("rt", "mob", None), P("rt", "mob")),
        check_vma=False,
    )
```

profile of v0, /device:TPU:0, one launch (start us, length us, event | category | flops | bytes accessed | tf_op | source)
XLA Modules:
  0.0 713.5 jit_solution(16873806584729619166)
XLA Ops:
  15.4 3.8 collective-permute-done.1
  19.9 15.1 %fusion.127 = f32[32,16,1280]{2,1,0:T(8,128)S(1)} fusion(f32[32,16,1280]{2,1,0:T(8,128)S(1)} %copy-done, f32[32,7,1280]{2,1,0:T(8,128)S(1)} %copy.17, f32[32,23,1280]{2,1,0:T(8,128)S(1)} %copy_dynamic-update-slice_fusion, f32[]{:T(128)} %bitcast.16, f32[]{:T(128)} %bitcast.15, f32[]{:T(128)} %bitcast.14, f32[]{:T(128)} %bitcast.13, f32[]{:T(128)} %bitcast.12, ...), kind=kLoop, calls=%fused_computation.435 | loop fusion | flops 23592960 | bytes 24739900 | tf_op jit(solution)/shard_map/add | solution.py:30
  41.3 46.4 %collective-permute-done.2 = f32[15,16,1280]{2,1,0:T(8,128)S(1)} collective-permute-done((f32[15,16,1280]{2,1,0:T(8,128)S(1)}, f32[15,16,1280]{2,1,0:T(8,128)S(1)}, u32[]{:S(2)}, u32[]{:S(2)}) %collective-permute-start.2) | collective-permute-done | bytes 1228832 | tf_op jit(solution)/shard_map/ppermute | solution.py:18
  88.8 34.5 %fusion.405 = f32[32,16,1280]{2,1,0:T(8,128)} fusion(f32[32,16,1280]{2,1,0:T(8,128)S(1)} %copy-done, f32[32,16,1280]{2,1,0:T(8,128)S(1)} %fusion.127, f32[15,16,1280]{2,1,0:T(8,128)} %copy-done.5, f32[15,16,1280]{2,1,0:T(8,128)S(1)} %collective-permute-done.2, f32[]{:T(128)} %bitcast.45, f32[]{:T(128)} %bitcast.44, f32[]{:T(128)} %bitcast.43, f32[]{:T(128)} %bitcast.42, ...), kind=kLoop, calls=%fused_computation.713 | loop fusion | flops 60293120 | bytes 10322044 | tf_op jit(solution)/shard_map/div | solution.py:48
  125.1 4.5 collective-permute-start.4
  130.9 48.9 %collective-permute-done.4 = f32[15,16,1280]{2,1,0:T(8,128)S(1)} collective-permute-done((f32[15,16,1280]{2,1,0:T(8,128)S(1)}, f32[15,16,1280]{2,1,0:T(8,128)S(1)}, u32[]{:S(2)}, u32[]{:S(2)}) %collective-permute-start.4) | collective-permute-done | bytes 1228832 | tf_op jit(solution)/shard_map/ppermute | solution.py:18
  179.8 53.8 %fusion.318 = f32[32,16,1280]{2,1,0:T(8,128)S(1)} fusion(f32[32,16,1280]{2,1,0:T(8,128)} %fusion.405, f32[15,16,1280]{2,1,0:T(8,128)} %collective-permute-done.5, f32[15,16,1280]{2,1,0:T(8,128)S(1)} %collective-permute-done.4, f32[]{:T(128)} %bitcast.45, f32[]{:T(128)} %bitcast.44, f32[]{:T(128)} %bitcast.43, f32[]{:T(128)} %bitcast.42, f32[]{:T(128)} %bitcast.41, ...), kind=kLoop, calls=%fused_computation.626 | loop fusion | flops 59637760 | bytes 7700604 | tf_op jit(solution)/shard_map/add | solution.py:30
  235.5 5.7 collective-permute-start.6
  247.2 16.5 %fusion.81 = f32[32,16,1280]{2,1,0:T(8,128)S(1)} fusion(f32[32,16,1280]{2,1,0:T(8,128)S(1)} %copy-done, f32[32,16,1280]{2,1,0:T(8,128)S(1)} %copy-done.3, f32[32,7,1280]{2,1,0:T(8,128)S(1)} %copy.23, f32[32,7,1280]{2,1,0:T(8,128)S(1)} %copy.21, f32[]{:T(128)} %bitcast.16, f32[]{:T(128)} %bitcast.15, f32[]{:T(128)} %bitcast.14, f32[]{:T(128)} %bitcast.13, ...), kind=kLoop, calls=%fused_computation.389 | loop fusion | flops 28835840 | bytes 10158140 | tf_op jit(solution)/shard_map/mul | solution.py:53
  264.3 14.4 %collective-permute-start.8 = (f32[32,7,1280]{2,0,1:T(8,128)S(1)}, f32[32,7,1280]{2,0,1:T(8,128)S(1)}, u32[]{:S(2)}, u32[]{:S(2)}) collective-permute-start(f32[32,7,1280]{2,0,1:T(8,128)S(1)} %copy.24), channel_id=1, source_target_pairs={{0,1},{1,2},{2,3},{4,5},{5,6},{6,7},{8,9},{9,10},{10,11},{12,13},{... | collective-permute-start | bytes 3440648 | tf_op jit(solution)/shard_map/ppermute | solution.py:18
  284.5 16.3 %fusion.42 = f32[32,16,1280]{2,1,0:T(8,128)S(1)} fusion(f32[32,16,1280]{2,1,0:T(8,128)S(1)} %fusion.81, f32[32,7,1280]{2,1,0:T(8,128)S(1)} %copy.27, f32[32,7,1280]{2,1,0:T(8,128)S(1)} %copy.25, f32[]{:T(128)} %bitcast.16, f32[]{:T(128)} %bitcast.15, f32[]{:T(128)} %bitcast.14, f32[]{:T(128)} %bitcast.13, f32[]{:T(128)} %bitcast.12, f32[]{:T(128)} %bitcast.11, ...), kind=kLoop, calls=%fused_computation.350 | loop fusion | flops 28180480 | bytes 7536700 | tf_op jit(solution)/shard_map/add | solution.py:30
  302.5 4.2 collective-permute-start.10
  307.9 42.2 %collective-permute-done.10 = f32[15,16,1280]{2,1,0:T(8,128)S(1)} collective-permute-done((f32[15,16,1280]{2,1,0:T(8,128)S(1)}, f32[15,16,1280]{2,1,0:T(8,128)S(1)}, u32[]{:S(2)}, u32[]{:S(2)}) %collective-permute-start.10) | collective-permute-done | bytes 1228832 | tf_op jit(solution)/shard_map/ppermute | solution.py:18
  350.1 54.3 %fusion.232 = f32[32,16,1280]{2,1,0:T(8,128)} fusion(f32[32,16,1280]{2,1,0:T(8,128)S(1)} %copy-done, f32[32,16,1280]{2,1,0:T(8,128)} %copy-done.4, f32[15,16,1280]{2,1,0:T(8,128)} %collective-permute-done.11, f32[15,16,1280]{2,1,0:T(8,128)S(1)} %collective-permute-done.10, f32[]{:T(128)} %bitcast.45, f32[]{:T(128)} %bitcast.44, f32[]{:T(128)} %bitcast.43, ...), kind=kLoop, calls=%fused_computation.540 | loop fusion | flops 60293120 | bytes 10322044 | tf_op jit(solution)/shard_map/div | solution.py:48
  406.3 4.5 collective-permute-start.12
  412.3 16.7 %collective-permute-done.12 = f32[15,16,1280]{2,1,0:T(8,128)S(1)} collective-permute-done((f32[15,16,1280]{2,1,0:T(8,128)S(1)}, f32[15,16,1280]{2,1,0:T(8,128)S(1)}, u32[]{:S(2)}, u32[]{:S(2)}) %collective-permute-start.12) | collective-permute-done | bytes 1228832 | tf_op jit(solution)/shard_map/ppermute | solution.py:18
  429.0 29.0 %collective-permute-done.13 = f32[15,16,1280]{2,1,0:T(8,128)} collective-permute-done((f32[15,16,1280]{2,1,0:T(8,128)S(1)}, f32[15,16,1280]{2,1,0:T(8,128)}, u32[]{:S(2)}, u32[]{:S(2)}) %collective-permute-start.13) | collective-permute-done | bytes 1228832 | tf_op jit(solution)/shard_map/ppermute | solution.py:20
  457.9 52.5 %fusion.145 = f32[32,16,1280]{2,1,0:T(8,128)S(1)} fusion(f32[32,16,1280]{2,1,0:T(8,128)} %fusion.232, f32[15,16,1280]{2,1,0:T(8,128)} %collective-permute-done.13, f32[15,16,1280]{2,1,0:T(8,128)S(1)} %collective-permute-done.12, f32[]{:T(128)} %bitcast.45, f32[]{:T(128)} %bitcast.44, f32[]{:T(128)} %bitcast.43, f32[]{:T(128)} %bitcast.42, f32[]{:T(128)} %bitcast.41, ...), kind=kLoop, calls=%fused_computation.453 | loop fusion | flops 59637760 | bytes 7700604 | tf_op jit(solution)/shard_map/add | solution.py:30
  511.1 8.6 %collective-permute-start.14 = (f32[32,7,1280]{2,0,1:T(8,128)S(1)}, f32[32,7,1280]{2,0,1:T(8,128)S(1)}, u32[]{:S(2)}, u32[]{:S(2)}) collective-permute-start(f32[32,7,1280]{2,0,1:T(8,128)S(1)} %copy.28), channel_id=1, source_target_pairs={{0,1},{1,2},{2,3},{4,5},{5,6},{6,7},{8,9},{9,10},{10,11},{12,13},{... | collective-permute-start | bytes 3440648 | tf_op jit(solution)/shard_map/ppermute | solution.py:18
  525.4 17.4 %fusion.507 = (f32[1280]{0:T(1024)S(1)}, f32[32,16,1280]{2,1,0:T(8,128)}) fusion(f32[32,16,1280]{2,1,0:T(8,128)S(1)} %fusion.81, f32[32,7,1280]{2,1,0:T(8,128)S(1)} %copy.31, f32[32,16,1280]{2,1,0:T(8,128)S(1)} %fusion.145, f32[]{:T(128)} %bitcast.3, f32[]{:T(128)} %bitcast.4, f32[]{:T(128)} %bitcast.5, f32[]{:T(128)} %bitcast.6, f32[]{:T(128)} %bitcast.7, ...), kind=kLoop, calls=%fused_computation.845 | loop fusion | flops 29489920 | bytes 10163260 | tf_op jit(solution)/shard_map/reduce_sum | solution.py:56
  542.8 67.7 %psum.14 = f32[1280]{0:T(1024)S(1)} all-reduce(f32[1280]{0:T(1024)S(1)} %get-tuple-element.4), channel_id=1, replica_groups=mesh['rt'=8,'mob'=4] {'rt','mob'}, use_global_device_ids=true, to_apply=%region_1.0 | all-reduce | flops 1280 | bytes 10240 | tf_op jit(solution)/shard_map/psum | solution.py:56
  614.0 26.2 %reduce-scatter.3.cloned.1.call-done = f32[256,256]{1,0:T(8,128)} async-done(((f32[256,1024]{1,0:T(8,128)}), f32[256,256]{1,0:T(8,128)}) %reduce-scatter.3.cloned.1.call-update) | async-done | bytes 262160 | tf_op jit(solution)/shard_map/reduce_scatter | solution.py:67
  640.6 39.5 %psum.15 = f32[1280]{0:T(1024)S(1)} all-reduce(f32[1280]{0:T(1024)S(1)} %multiply_reduce_fusion), channel_id=1, replica_groups=mesh['rt'=8,'mob'=4] {'rt','mob'}, use_global_device_ids=true, to_apply=%region_5.0 | all-reduce | flops 1280 | bytes 10240 | tf_op jit(solution)/shard_map/psum | solution.py:60
  680.3 24.9 %reduce-scatter.5.cloned.1.call-done = f32[32,256]{1,0:T(8,128)} async-done(((f32[256,256]{1,0:T(8,128)}), f32[32,256]{1,0:T(8,128)}) %reduce-scatter.5.cloned.1.call-update) | async-done | bytes 32784 | tf_op jit(solution)/shard_map/reduce_scatter | solution.py:68
  (82 shorter events, 51.5 us)
Async XLA Ops:
  7.2 633.1 %reduce-scatter.3.cloned.1.call-start = ((), (), s32[]{:S(2)}) async-start(), calls=%async_computation.2 | async-start | bytes 1310720 | tf_op jit(solution)/shard_map/reduce_scatter | solution.py:67
  9.1 5.4 copy-start
  9.5 5.2 collective-permute-start
  12.4 6.7 collective-permute-start.1
  34.9 5.0 copy-start.6
  35.1 52.7 %collective-permute-start.2 = (f32[15,16,1280]{2,1,0:T(8,128)S(1)}, f32[15,16,1280]{2,1,0:T(8,128)S(1)}, u32[]{:S(2)}, u32[]{:S(2)}) collective-permute-start(f32[15,16,1280]{2,1,0:T(8,128)S(1)} %get-tuple-element.18), channel_id=1, source_target_pairs={{0,4},{4,8},{8,12},{12,16},{16,20},{20,24},{24,28},{1,5},{5,9},{9,... | collective-permute-start | bytes 3686408 | tf_op jit(solution)/shard_map/ppermute | solution.py:18
  38.6 49.2 %collective-permute-start.3 = (f32[15,16,1280]{2,1,0:T(8,128)S(1)}, f32[15,16,1280]{2,1,0:T(8,128)S(1)}, u32[]{:S(2)}, u32[]{:S(2)}) collective-permute-start(f32[15,16,1280]{2,1,0:T(8,128)S(1)} %get-tuple-element.19), channel_id=1, source_target_pairs={{4,0},{8,4},{12,8},{16,12},{20,16},{24,20},{28,24},{5,1},{9,5},{13... | collective-permute-start | bytes 3686408 | tf_op jit(solution)/shard_map/ppermute | solution.py:20
  125.1 54.7 %collective-permute-start.4 = (f32[15,16,1280]{2,1,0:T(8,128)S(1)}, f32[15,16,1280]{2,1,0:T(8,128)S(1)}, u32[]{:S(2)}, u32[]{:S(2)}) collective-permute-start(f32[15,16,1280]{2,1,0:T(8,128)S(1)} %get-tuple-element.16), channel_id=1, source_target_pairs={{0,4},{4,8},{8,12},{12,16},{16,20},{20,24},{24,28},{1,5},{5,9},{9,... | collective-permute-start | bytes 3686408 | tf_op jit(solution)/shard_map/ppermute | solution.py:18
  129.6 50.2 %collective-permute-start.5 = (f32[15,16,1280]{2,1,0:T(8,128)S(1)}, f32[15,16,1280]{2,1,0:T(8,128)}, u32[]{:S(2)}, u32[]{:S(2)}) collective-permute-start(f32[15,16,1280]{2,1,0:T(8,128)S(1)} %get-tuple-element.17), channel_id=1, source_target_pairs={{4,0},{8,4},{12,8},{16,12},{20,16},{24,20},{28,24},{5,1},{9,5},{13... | collective-permute-start | bytes 3686408 | tf_op jit(solution)/shard_map/ppermute | solution.py:20
  235.5 7.9 %collective-permute-start.6 = (f32[32,7,1280]{2,0,1:T(8,128)S(1)}, f32[32,7,1280]{2,0,1:T(8,128)S(1)}, u32[]{:S(2)}, u32[]{:S(2)}) collective-permute-start(f32[32,7,1280]{2,0,1:T(8,128)S(1)} %copy.20), channel_id=1, source_target_pairs={{0,1},{1,2},{2,3},{4,5},{5,6},{6,7},{8,9},{9,10},{10,11},{12,13},{... | collective-permute-start | bytes 3440648 | tf_op jit(solution)/shard_map/ppermute | solution.py:18
  241.6 5.7 copy-start.3
  241.6 5.0 collective-permute-start.7
  264.3 16.7 %collective-permute-start.8 = (f32[32,7,1280]{2,0,1:T(8,128)S(1)}, f32[32,7,1280]{2,0,1:T(8,128)S(1)}, u32[]{:S(2)}, u32[]{:S(2)}) collective-permute-start(f32[32,7,1280]{2,0,1:T(8,128)S(1)} %copy.24), channel_id=1, source_target_pairs={{0,1},{1,2},{2,3},{4,5},{5,6},{6,7},{8,9},{9,10},{10,11},{12,13},{... | collective-permute-start | bytes 3440648 | tf_op jit(solution)/shard_map/ppermute | solution.py:18
  279.1 4.7 collective-permute-start.9
  302.5 47.7 %collective-permute-start.10 = (f32[15,16,1280]{2,1,0:T(8,128)S(1)}, f32[15,16,1280]{2,1,0:T(8,128)S(1)}, u32[]{:S(2)}, u32[]{:S(2)}) collective-permute-start(f32[15,16,1280]{2,1,0:T(8,128)S(1)} %get-tuple-element.10), channel_id=1, source_target_pairs={{0,4},{4,8},{8,12},{12,16},{16,20},{20,24},{24,28},{1,5},{5,9},{9,... | collective-permute-start | bytes 3686408 | tf_op jit(solution)/shard_map/ppermute | solution.py:18
  306.6 43.5 %collective-permute-start.11 = (f32[15,16,1280]{2,1,0:T(8,128)S(1)}, f32[15,16,1280]{2,1,0:T(8,128)}, u32[]{:S(2)}, u32[]{:S(2)}) collective-permute-start(f32[15,16,1280]{2,1,0:T(8,128)S(1)} %get-tuple-element.11), channel_id=1, source_target_pairs={{4,0},{8,4},{12,8},{16,12},{20,16},{24,20},{28,24},{5,1},{9,5},{13... | collective-permute-start | bytes 3686408 | tf_op jit(solution)/shard_map/ppermute | solution.py:20
  406.3 22.7 %collective-permute-start.12 = (f32[15,16,1280]{2,1,0:T(8,128)S(1)}, f32[15,16,1280]{2,1,0:T(8,128)S(1)}, u32[]{:S(2)}, u32[]{:S(2)}) collective-permute-start(f32[15,16,1280]{2,1,0:T(8,128)S(1)} %get-tuple-element.8), channel_id=1, source_target_pairs={{0,4},{4,8},{8,12},{12,16},{16,20},{20,24},{24,28},{1,5},{5,9},{9,... | collective-permute-start | bytes 3686408 | tf_op jit(solution)/shard_map/ppermute | solution.py:18
  410.7 47.2 %collective-permute-start.13 = (f32[15,16,1280]{2,1,0:T(8,128)S(1)}, f32[15,16,1280]{2,1,0:T(8,128)}, u32[]{:S(2)}, u32[]{:S(2)}) collective-permute-start(f32[15,16,1280]{2,1,0:T(8,128)S(1)} %get-tuple-element.9), channel_id=1, source_target_pairs={{4,0},{8,4},{12,8},{16,12},{20,16},{24,20},{28,24},{5,1},{9,5},{13... | collective-permute-start | bytes 3686408 | tf_op jit(solution)/shard_map/ppermute | solution.py:20
  511.1 10.9 %collective-permute-start.14 = (f32[32,7,1280]{2,0,1:T(8,128)S(1)}, f32[32,7,1280]{2,0,1:T(8,128)S(1)}, u32[]{:S(2)}, u32[]{:S(2)}) collective-permute-start(f32[32,7,1280]{2,0,1:T(8,128)S(1)} %copy.28), channel_id=1, source_target_pairs={{0,1},{1,2},{2,3},{4,5},{5,6},{6,7},{8,9},{9,10},{10,11},{12,13},{... | collective-permute-start | bytes 3440648 | tf_op jit(solution)/shard_map/ppermute | solution.py:18
  520.0 4.7 collective-permute-start.15
  612.5 27.9 %copy-start.1 = (f32[32,16,1280]{2,1,0:T(8,128)S(1)}, f32[32,16,1280]{2,1,0:T(8,128)}, u32[]{:S(2)}) copy-start(f32[32,16,1280]{2,1,0:T(8,128)} %get-tuple-element.5) | copy-start | bytes 7864324
  612.5 92.8 %copy-start.8 = (s32[256]{0:T(256)S(1)}, s32[256]{0:T(256)}, u32[]{:S(2)}) copy-start(s32[256]{0:T(256)} %param.9) | copy-start | bytes 3076
  612.5 92.8 %copy-start.9 = (s32[32]{0:T(128)S(1)}, s32[32]{0:T(128)}, u32[]{:S(2)}) copy-start(s32[32]{0:T(128)} %param.8) | copy-start | bytes 388
  614.0 91.3 %reduce-scatter.5.cloned.1.call-start = ((), (), s32[]{:S(2)}) async-start(), calls=%async_computation.3 | async-start | bytes 294912 | tf_op jit(solution)/shard_map/reduce_scatter | solution.py:68
  (4 other events, 8.7 us)
Sparse Core Ops, SparseCore 0:
  614.1 26.1 reduce-scatter.2
  644.0 61.2 reduce-scatter.4
where the time goes:
time: 716 us; the launch traced here: 714 us
  other arithmetic  264 us (37%)
  waiting for transfers between devices  246 us (34%)
  blocking collectives  107 us (15%)
  starting transfers between devices  58.7 us (8%)
  local copies, waits for them, and re-layouts  21.2 us (3%)
  between operations  14.5 us (2%)
    ppermute x8, waiting for transfers between devices, extended(): lax.ppermute(tail, axis, [(i, (i + 1) % count) for i in range(ends)])  156 us
    add x4, other arithmetic, apply_taps(): running + kernel[tap_index] * lax.slice_in_dim(padded, tap_index, tap_ind...  138 us
    div x2, other arithmetic, local(): ratio_field = observed / blurred_image  88.8 us
    psum x1, blocking collectives, local(): channel_total = lax.psum(jnp.sum(profiles, axis=0), ('rt', 'mob'))  67.7 us
    ppermute x8, starting transfers between devices, extended(): lax.ppermute(tail, axis, [(i, (i + 1) % count) for i in range(ends)])  47.8 us
    psum x1, blocking collectives, local(): squares = lax.psum(jnp.sum(as_float * as_float, axis=0), ('rt', 'mob'))  39.5 us
    ppermute x8, waiting for transfers between devices, extended(): lax.ppermute(head, axis, [((i + 1) % count, i) for i in range(ends)])  39.4 us
    reduce_scatter x1, waiting for transfers between devices, local(): lax.psum_scatter(cross_sums, 'mob', scatter_dimension=1, tiled=True)  26.2 us
  transfers between devices with their start and end apart: 18, of which 14 were waited for; matrix products, arithmetic and copies ran while one was open for 1% of the time, Pallas kernels for 0%

commit v1 on v0

v1 whole, which is shorter than its diff:
```python
import functools

import jax
import jax.numpy as jnp
from jax import lax
from jax.experimental import pallas as pl
from jax.experimental.pallas import tpu as pltpu
from jax.sharding import PartitionSpec as P

PREC = 256
ITERS = 2
LANES = 128
SUB = 8
STEP = 16


def scan_taps(pad_ref, frame, taps, scans):
    radius = (len(taps) - 1) // 2
    total = None
    for a, tap in enumerate(taps):
        part = tap * pad_ref[frame, pl.ds(SUB - radius + a, scans), :]
        total = part if total is None else total + part
    return total


def scan_kernel_body(flip, k_ref, mid_ref, lo_ref, hi_ref, *rest):
    *scale, out_ref, pad_ref = rest
    frames, scans, _ = mid_ref.shape
    count = k_ref.shape[0]
    taps = [k_ref[count - 1 - a if flip else a] for a in range(count)]
    pad_ref[:, :SUB, :] = lo_ref[...]
    pad_ref[:, SUB : SUB + scans, :] = mid_ref[...]
    pad_ref[:, SUB + scans :, :] = hi_ref[...]

    def one(frame, carry):
        total = scan_taps(pad_ref, frame, taps, scans)
        if scale:
            total = scale[0][frame] * total
        out_ref[frame] = total
        return carry

    lax.fori_loop(0, frames, one, 0, unroll=4)


def frame_kernel_body(flip, divide, k_ref, mid_ref, lo_ref, hi_ref, *rest):
    *above, out_ref, pad_ref = rest
    frames, scans, _ = mid_ref.shape
    count = k_ref.shape[0]
    radius = (count - 1) // 2
    pad_ref[:radius] = lo_ref[...]
    pad_ref[radius : radius + frames] = mid_ref[...]
    pad_ref[radius + frames :] = hi_ref[...]
    taps = [
        jnp.full((SUB, LANES), k_ref[count - 1 - a if flip else a], jnp.float32)
        for a in range(count)
    ]
    rows_of = scans // SUB

    def block(index, carry):
        first = (index // rows_of) * STEP
        rows = pl.ds(pl.multiple_of((index % rows_of) * SUB, SUB), SUB)
        totals = [None] * STEP
        for j in range(STEP + count - 1):
            value = pad_ref[first + j, rows, :]
            for i in range(STEP):
                if 0 <= j - i < count:
                    part = taps[j - i] * value
                    totals[i] = part if totals[i] is None else totals[i] + part
        for i in range(STEP):
            result = totals[i]
            if divide:
                result = above[0][first + i, rows, :] / result
            out_ref[first + i, rows, :] = result
        return carry

    lax.fori_loop(0, (frames // STEP) * rows_of, block, 0)


def blur(body, taps, arrays, pad_shape):
    frames, scans, channels = arrays[0].shape

    def spec(array):
        return pl.BlockSpec((array.shape[0], array.shape[1], LANES), lambda c: (0, 0, c))

    return pl.pallas_call(
        body,
        grid=(channels // LANES,),
        in_specs=[pl.BlockSpec(memory_space=pltpu.SMEM)] + [spec(a) for a in arrays],
        out_specs=pl.BlockSpec((frames, scans, LANES), lambda c: (0, 0, c)),
        out_shape=jax.ShapeDtypeStruct((frames, scans, channels), jnp.float32),
        scratch_shapes=[pltpu.VMEM(pad_shape, jnp.float32)],
        compiler_params=pltpu.CompilerParams(vmem_limit_bytes=32 * 1024 * 1024),
        cost_estimate=pl.CostEstimate(
            flops=2 * taps.shape[0] * frames * scans * channels,
            bytes_accessed=12 * frames * scans * channels,
            transcendentals=0,
        ),
    )(taps, *arrays)


def halo(cells, axis, dim, width, hop):
    count = lax.axis_size(axis)
    size = cells.shape[dim]
    up = [(i, i + hop) for i in range(count - hop)]
    down = [(i + hop, i) for i in range(count - hop)]
    before = lax.ppermute(lax.slice_in_dim(cells, size - width, size, axis=dim), axis, up)
    after = lax.ppermute(lax.slice_in_dim(cells, 0, width, axis=dim), axis, down)
    return before, after


def local(observed, frame_kernel, scan_kernel, prec_window, frag_window):
    frames, scan_count, channels = observed.shape
    radius = (frame_kernel.shape[0] - 1) // 2
    half = channels // 2
    count = lax.axis_size("rt")
    side = lax.rem(lax.axis_index("rt"), 2)
    swap = [(i, i ^ 1) for i in range(count)]

    def blur_scans(flip, cells, *scale):
        before, after = halo(cells, "mob", 1, SUB, 1)
        return blur(
            functools.partial(scan_kernel_body, flip),
            scan_kernel,
            (cells, before, after) + scale,
            (cells.shape[0], scan_count + 2 * SUB, LANES),
        )

    def blur_frames(flip, cells, *above):
        before, after = halo(cells, "rt", 0, radius, 2)
        return blur(
            functools.partial(frame_kernel_body, flip, bool(above)),
            frame_kernel,
            (cells, before, after) + above,
            (cells.shape[0] + 2 * radius, scan_count, LANES),
        )

    mine = lax.dynamic_slice_in_dim(observed, side * half, half, axis=2)
    other = lax.dynamic_slice_in_dim(observed, (1 - side) * half, half, axis=2)
    other = lax.ppermute(other, "rt", swap)
    first = side == 0
    wide = jnp.concatenate([jnp.where(first, mine, other), jnp.where(first, other, mine)], axis=0)
    estimate = wide
    for iteration in range(ITERS):
        ratio = blur_frames(False, blur_scans(False, estimate), wide)
        estimate = blur_scans(True, blur_frames(True, ratio), estimate)
    mine = lax.dynamic_slice_in_dim(estimate, side * frames, frames, axis=0)
    other = lax.dynamic_slice_in_dim(estimate, (1 - side) * frames, frames, axis=0)
    other = lax.ppermute(other, "rt", swap)
    estimate = jnp.concatenate(
        [jnp.where(first, mine, other), jnp.where(first, other, mine)], axis=2
    )
    profiles = estimate.reshape(frames * scan_count, channels)
    cell_count = frames * scan_count * lax.axis_size("rt") * lax.axis_size("mob")
    channel_total = lax.psum(jnp.sum(profiles, axis=0), ("rt", "mob"))
    channel_mean = channel_total / cell_count
    centered = (profiles - channel_mean).astype(jnp.bfloat16)
    as_float = centered.astype(jnp.float32)
    squares = lax.psum(jnp.sum(as_float * as_float, axis=0), ("rt", "mob"))
    cross_sums = lax.dot_general(
        centered[:, :PREC],
        centered[:, PREC:],
        (((0,), (0,)), ((), ())),
        preferred_element_type=jnp.float32,
    )
    partial_value = lax.psum_scatter(cross_sums, "mob", scatter_dimension=1, tiled=True)
    block_sums = lax.psum_scatter(partial_value, "rt", scatter_dimension=0, tiled=True)
    row_count = prec_window.shape[0]
    column_count = frag_window.shape[0]
    inverse_norm = 1.0 / jnp.sqrt(squares + 1e-06)
    row_inverse = lax.dynamic_slice_in_dim(
        inverse_norm[:PREC], lax.axis_index("rt") * row_count, row_count
    )
    column_inverse = lax.dynamic_slice_in_dim(
        inverse_norm[PREC:], lax.axis_index("mob") * column_count, column_count
    )
    pair_mask = (prec_window[:, None] == frag_window[None, :]).astype(jnp.float32)
    correlation = pair_mask * block_sums * row_inverse[:, None] * column_inverse[None, :]
    return (estimate, correlation)


def solution(mesh):
    placed = (P("rt", "mob", None), P(), P(), P("rt"), P("mob"))
    return jax.shard_map(
        local,
        mesh=mesh,
        in_specs=placed,
        out_specs=(P("rt", "mob", None), P("rt", "mob")),
        check_vma=False,
    )
```

time: 716 us -> 405 us (0.57)
  other arithmetic: 264 us -> 5.7 us
  waiting for transfers between devices: 246 us -> 135 us
  Pallas kernels: 0 us -> 52 us
  starting transfers between devices: 58.7 us -> 86.7 us
  local copies, waits for them, and re-layouts: 21.2 us -> 9.05 us
  blocking collectives: 107 us -> 99.4 us
    add x4 -> x0, other arithmetic: 138 us -> none  [apply_taps(): running + kernel[tap_index] * lax.slice_in_dim(padded, tap_index, tap_ind...]
    ppermute x16 -> x18, waiting for transfers between devices: 195 us -> 85 us  [the longest x2 45.1 us: local(): other = lax.ppermute(other, 'rt', swap)]
    div x2 -> x0, other arithmetic: 88.8 us -> none  [local(): ratio_field = observed / blurred_image]
    pallas_call x0 -> x8, Pallas kernels: none -> 52 us  [blur(): pl.pallas_call(body, grid=(channels // LANES,), in_specs=[pl.BlockSpec(me...]
    ppermute x16 -> x18, starting transfers between devices: 58.6 us -> 86.6 us  [the longest x8 71.8 us: halo(): lax.ppermute(lax.slice_in_dim(cells, size - width, size, axis=dim), axis,...]
    reduce_sum x1, other arithmetic: 17.4 us -> 0.41 us  [local(): channel_total = lax.psum(jnp.sum(profiles, axis=0), ('rt', 'mob'))]
    mul x1 -> x0, other arithmetic: 16.5 us -> none  [local(): estimate * apply_taps(scan_padded_scans, flip_scans, 1, scan_count)]
    slice x17 -> x7, local copies, waits for them, and re-layouts: 10.8 us -> 2.46 us  [halo(): lax.slice_in_dim(cells, 0, width, axis=dim)]
  transfers between devices with their start and end apart: 18 -> 20, of which waited for: 14 -> 19; matrix products, arithmetic and copies ran while one was open for 1% -> 0% of each run, Pallas kernels for 0% -> 0%
where the time goes in v1:
time: 405 us; the launch traced here: 404 us
  waiting for transfers between devices  135 us (33%)
  blocking collectives  99.4 us (25%)
  starting transfers between devices  86.7 us (21%)
  Pallas kernels  52 us (13%)
  between operations  14.4 us (4%)
  local copies, waits for them, and re-layouts  9.05 us (2%)
  other arithmetic  5.7 us (1%)
    ppermute x8, starting transfers between devices, halo(): lax.ppermute(lax.slice_in_dim(cells, size - width, size, axis=dim), axis,...  71.8 us
    psum x1, blocking collectives, local(): channel_total = lax.psum(jnp.sum(profiles, axis=0), ('rt', 'mob'))  59.8 us
    pallas_call x8, Pallas kernels, blur(): pl.pallas_call(body, grid=(channels // LANES,), in_specs=[pl.BlockSpec(me...  52 us
    ppermute x2, waiting for transfers between devices, local(): other = lax.ppermute(other, 'rt', swap)  45.1 us
    psum x1, blocking collectives, local(): squares = lax.psum(jnp.sum(as_float * as_float, axis=0), ('rt', 'mob'))  39.5 us
    ppermute x8, waiting for transfers between devices, halo(): lax.ppermute(lax.slice_in_dim(cells, 0, width, axis=dim), axis, down)  25.9 us
    reduce_scatter x1, waiting for transfers between devices, local(): lax.psum_scatter(cross_sums, 'mob', scatter_dimension=1, tiled=True)  25.3 us
    reduce_scatter x1, waiting for transfers between devices, local(): lax.psum_scatter(partial_value, 'rt', scatter_dimension=0, tiled=True)  24.9 us
  transfers between devices with their start and end apart: 20, of which 19 were waited for; matrix products, arithmetic and copies ran while one was open for 0% of the time, Pallas kernels for 0%

profile of v1, /device:TPU:0, one launch (start us, length us, event | category | flops | bytes accessed | tf_op | source)
XLA Modules:
  0.0 403.9 jit_solution(6736035363365502327)
XLA Ops:
  12.8 29.1 %collective-permute-done = f32[32,16,640]{2,1,0:T(8,128)} collective-permute-done((f32[32,16,640]{2,1,0:T(8,128)}, f32[32,16,640]{2,1,0:T(8,128)}, u32[]{:S(2)}, u32[]{:S(2)}) %collective-permute-start) | collective-permute-done | bytes 1310752 | tf_op jit(solution)/shard_map/ppermute | solution.py:139
  50.6 4.8 %shard_map.68.mid_ref = f32[64,16,640]{2,1,0:T(8,128)S(1)} custom-call(f32[15]{0:T(128)S(1)} %copy-done.4, f32[64,16,640]{2,1,0:T(8,128)S(1)} %pad_maximum_fusion.mid_ref.rest_0_, f32[64,8,640]{2,1,0:T(8,128)S(1)} %collective-permute-done.1.lo_ref, f32[64,8,640]{2,1,0:T(8,128)S(1)} %collective-permute-done.2.hi_ref), custom_call_target="tpu_custom_call" | custom-call | flops 19660800 | bytes 7864320 | tf_op jit(solution)/shard_map/pallas_call | solution.py:85
  61.4 6.1 %collective-permute-done.4.hi_ref = f32[15,16,640]{2,1,0:T(8,128)S(1)} collective-permute-done((f32[15,16,640]{2,1,0:T(8,128)S(1)}, f32[15,16,640]{2,1,0:T(8,128)S(1)}, u32[]{:S(2)}, u32[]{:S(2)}) %collective-permute-start.4) | collective-permute-done | bytes 614432 | tf_op jit(solution)/shard_map/ppermute | solution.py:107
  69.0 8.2 %shard_map.69.mid_ref = f32[64,16,640]{2,1,0:T(8,128)S(1)} custom-call(f32[31]{0:T(128)S(1)} %copy-done.3, f32[64,16,640]{2,1,0:T(8,128)S(1)} %shard_map.68.mid_ref, f32[15,16,640]{2,1,0:T(8,128)S(1)} %collective-permute-done.3.lo_ref, f32[15,16,640]{2,1,0:T(8,128)S(1)} %collective-permute-done.4.hi_ref, f32[64,16,640]{2,1,0:T(8,128)S(1)} %pad_maximum_fusion.mid_ref.rest_0_), custom_call_target="tpu_custom_call" | custom-call | flops 40632320 | bytes 7864320 | tf_op jit(solution)/shard_map/pallas_call | solution.py:85
  78.6 5.1 %collective-permute-start.5 = (f32[15,16,640]{2,1,0:T(8,128)S(1)}, f32[15,16,640]{2,1,0:T(8,128)S(1)}, u32[]{:S(2)}, u32[]{:S(2)}) collective-permute-start(f32[15,16,640]{2,1,0:T(8,128)S(1)} %get-tuple-element.19), channel_id=1, source_target_pairs={{0,8},{4,12},{8,16},{12,20},{16,24},{20,28},{1,9},{5,13},{9,17},{1... | collective-permute-start | bytes 1843208 | tf_op jit(solution)/shard_map/ppermute | solution.py:106
  83.7 6.1 %collective-permute-done.6.hi_ref = f32[15,16,640]{2,1,0:T(8,128)S(1)} collective-permute-done((f32[15,16,640]{2,1,0:T(8,128)S(1)}, f32[15,16,640]{2,1,0:T(8,128)S(1)}, u32[]{:S(2)}, u32[]{:S(2)}) %collective-permute-start.6) | collective-permute-done | bytes 614432 | tf_op jit(solution)/shard_map/ppermute | solution.py:107
  91.3 7.6 %shard_map.70.mid_ref = f32[64,16,640]{2,1,0:T(8,128)S(1)} custom-call(f32[31]{0:T(128)S(1)} %copy-done.3, f32[64,16,640]{2,1,0:T(8,128)S(1)} %shard_map.69.mid_ref, f32[15,16,640]{2,1,0:T(8,128)S(1)} %collective-permute-done.5.lo_ref, f32[15,16,640]{2,1,0:T(8,128)S(1)} %collective-permute-done.6.hi_ref), custom_call_target="tpu_custom_call" | custom-call | flops 40632320 | bytes 7864320 | tf_op jit(solution)/shard_map/pallas_call | solution.py:85
  100.3 13.6 %collective-permute-start.7 = (f32[64,8,640]{2,1,0:T(8,128)S(1)}, f32[64,8,640]{2,1,0:T(8,128)S(1)}, u32[]{:S(2)}, u32[]{:S(2)}) collective-permute-start(f32[64,8,640]{2,1,0:T(8,128)S(1)} %get-tuple-element.17), channel_id=1, source_target_pairs={{0,1},{1,2},{2,3},{4,5},{5,6},{6,7},{8,9},{9,10},{10,11},{12,13},{... | collective-permute-start | bytes 3932168 | tf_op jit(solution)/shard_map/ppermute | solution.py:106
  116.4 5.2 %shard_map.71.mid_ref.rest_0_ = f32[64,16,640]{2,1,0:T(8,128)S(1)} custom-call(f32[15]{0:T(128)S(1)} %copy-done.4, f32[64,16,640]{2,1,0:T(8,128)S(1)} %shard_map.70.mid_ref, f32[64,8,640]{2,1,0:T(8,128)S(1)} %collective-permute-done.7.lo_ref, f32[64,8,640]{2,1,0:T(8,128)S(1)} %collective-permute-done.8.hi_ref, f32[64,16,640]{2,1,0:T(8,128)S(1)} %pad_maximum_fusion.mid_ref.rest_0_), custom_call_target="tpu_custom_call" | custom-call | flops 19660800 | bytes 7864320 | tf_op jit(solution)/shard_map/pallas_call | solution.py:85
  123.1 19.4 %collective-permute-start.9 = (f32[64,8,640]{2,1,0:T(8,128)S(1)}, f32[64,8,640]{2,1,0:T(8,128)S(1)}, u32[]{:S(2)}, u32[]{:S(2)}) collective-permute-start(f32[64,8,640]{2,1,0:T(8,128)S(1)} %get-tuple-element.15), channel_id=1, source_target_pairs={{0,1},{1,2},{2,3},{4,5},{5,6},{6,7},{8,9},{9,10},{10,11},{12,13},{... | collective-permute-start | bytes 3932168 | tf_op jit(solution)/shard_map/ppermute | solution.py:106
  145.0 4.8 %shard_map.72.mid_ref = f32[64,16,640]{2,1,0:T(8,128)S(1)} custom-call(f32[15]{0:T(128)S(1)} %copy-done.4, f32[64,16,640]{2,1,0:T(8,128)S(1)} %shard_map.71.mid_ref.rest_0_, f32[64,8,640]{2,1,0:T(8,128)S(1)} %collective-permute-done.9.lo_ref, f32[64,8,640]{2,1,0:T(8,128)S(1)} %collective-permute-done.10.hi_ref), custom_call_target="tpu_custom_call" | custom-call | flops 19660800 | bytes 7864320 | tf_op jit(solution)/shard_map/pallas_call | solution.py:85
  151.2 5.1 %collective-permute-start.11 = (f32[15,16,640]{2,1,0:T(8,128)S(1)}, f32[15,16,640]{2,1,0:T(8,128)S(1)}, u32[]{:S(2)}, u32[]{:S(2)}) collective-permute-start(f32[15,16,640]{2,1,0:T(8,128)S(1)} %get-tuple-element.13), channel_id=1, source_target_pairs={{0,8},{4,12},{8,16},{12,20},{16,24},{20,28},{1,9},{5,13},{9,17},{1... | collective-permute-start | bytes 1843208 | tf_op jit(solution)/shard_map/ppermute | solution.py:106
  156.3 6.1 %collective-permute-done.12.hi_ref = f32[15,16,640]{2,1,0:T(8,128)S(1)} collective-permute-done((f32[15,16,640]{2,1,0:T(8,128)S(1)}, f32[15,16,640]{2,1,0:T(8,128)S(1)}, u32[]{:S(2)}, u32[]{:S(2)}) %collective-permute-start.12) | collective-permute-done | bytes 614432 | tf_op jit(solution)/shard_map/ppermute | solution.py:107
  163.9 8.2 %shard_map.73.mid_ref = f32[64,16,640]{2,1,0:T(8,128)S(1)} custom-call(f32[31]{0:T(128)S(1)} %copy-done.3, f32[64,16,640]{2,1,0:T(8,128)S(1)} %shard_map.72.mid_ref, f32[15,16,640]{2,1,0:T(8,128)S(1)} %collective-permute-done.11.lo_ref, f32[15,16,640]{2,1,0:T(8,128)S(1)} %collective-permute-done.12.hi_ref, f32[64,16,640]{2,1,0:T(8,128)S(1)} %pad_maximum_fusion.mid_ref.rest_0_), custom_call_target="tpu_custom_call" | custom-call | flops 40632320 | bytes 7864320 | tf_op jit(solution)/shard_map/pallas_call | solution.py:85
  173.5 5.1 %collective-permute-start.13 = (f32[15,16,640]{2,1,0:T(8,128)S(1)}, f32[15,16,640]{2,1,0:T(8,128)S(1)}, u32[]{:S(2)}, u32[]{:S(2)}) collective-permute-start(f32[15,16,640]{2,1,0:T(8,128)S(1)} %get-tuple-element.11), channel_id=1, source_target_pairs={{0,8},{4,12},{8,16},{12,20},{16,24},{20,28},{1,9},{5,13},{9,17},{1... | collective-permute-start | bytes 1843208 | tf_op jit(solution)/shard_map/ppermute | solution.py:106
  178.6 6.1 %collective-permute-done.14.hi_ref = f32[15,16,640]{2,1,0:T(8,128)S(1)} collective-permute-done((f32[15,16,640]{2,1,0:T(8,128)S(1)}, f32[15,16,640]{2,1,0:T(8,128)S(1)}, u32[]{:S(2)}, u32[]{:S(2)}) %collective-permute-start.14) | collective-permute-done | bytes 614432 | tf_op jit(solution)/shard_map/ppermute | solution.py:107
  186.2 7.6 %shard_map.74.mid_ref = f32[64,16,640]{2,1,0:T(8,128)S(1)} custom-call(f32[31]{0:T(128)S(1)} %copy-done.3, f32[64,16,640]{2,1,0:T(8,128)S(1)} %shard_map.73.mid_ref, f32[15,16,640]{2,1,0:T(8,128)S(1)} %collective-permute-done.13.lo_ref, f32[15,16,640]{2,1,0:T(8,128)S(1)} %collective-permute-done.14.hi_ref), custom_call_target="tpu_custom_call" | custom-call | flops 40632320 | bytes 7864320 | tf_op jit(solution)/shard_map/pallas_call | solution.py:85
  197.4 16.0 %collective-permute-start.15 = (f32[64,8,640]{2,1,0:T(8,128)}, f32[64,8,640]{2,1,0:T(8,128)}, u32[]{:S(2)}, u32[]{:S(2)}) collective-permute-start(f32[64,8,640]{2,1,0:T(8,128)} %get-tuple-element.9), channel_id=1, source_target_pairs={{0,1},{1,2},{2,3},{4,5},{5,6},{6,7},{8,9},{9,10},{10,11},{12,13},{... | collective-permute-start | bytes 3932168 | tf_op jit(solution)/shard_map/ppermute | solution.py:106
  217.0 5.7 %shard_map.75 = f32[64,16,640]{2,1,0:T(8,128)S(1)} custom-call(f32[15]{0:T(128)S(1)} %copy-done.4, f32[64,16,640]{2,1,0:T(8,128)S(1)} %copy-done.1, f32[64,8,640]{2,1,0:T(8,128)} %collective-permute-done.15.lo_ref, f32[64,8,640]{2,1,0:T(8,128)} %collective-permute-done.16.hi_ref, f32[64,16,640]{2,1,0:T(8,128)S(1)} %shard_map.71.mid_ref.rest_0_), custom_call_target="tpu_custom_call" | custom-call | flops 19660800 | bytes 7864320 | tf_op jit(solution)/shard_map/pallas_call | solution.py:85
  225.8 16.0 %collective-permute-done.17 = f32[32,16,640]{2,1,0:T(8,128)S(1)} collective-permute-done((f32[32,16,640]{2,1,0:T(8,128)S(1)}, f32[32,16,640]{2,1,0:T(8,128)S(1)}, u32[]{:S(2)}, u32[]{:S(2)}) %collective-permute-start.17) | collective-permute-done | bytes 1310752 | tf_op jit(solution)/shard_map/ppermute | solution.py:148
  243.8 59.8 %psum.14 = f32[1280]{0:T(1024)S(1)} all-reduce(f32[1280]{0:T(1024)S(1)} %get-tuple-element.2), channel_id=1, replica_groups=mesh['rt'=8,'mob'=4] {'rt','mob'}, use_global_device_ids=true, to_apply=%region_1.2 | all-reduce | flops 1280 | bytes 10240 | tf_op jit(solution)/shard_map/psum | solution.py:154
  305.3 25.3 %reduce-scatter.3.cloned.1.call-done = f32[256,256]{1,0:T(8,128)} async-done(((f32[256,1024]{1,0:T(8,128)}), f32[256,256]{1,0:T(8,128)}) %reduce-scatter.3.cloned.1.call-update) | async-done | bytes 262160 | tf_op jit(solution)/shard_map/reduce_scatter | solution.py:165
  331.1 39.5 %psum.15 = f32[1280]{0:T(1024)S(1)} all-reduce(f32[1280]{0:T(1024)S(1)} %multiply_reduce_fusion), channel_id=1, replica_groups=mesh['rt'=8,'mob'=4] {'rt','mob'}, use_global_device_ids=true, to_apply=%region_5.6 | all-reduce | flops 1280 | bytes 10240 | tf_op jit(solution)/shard_map/psum | solution.py:158
  370.7 24.9 %reduce-scatter.5.cloned.1.call-done = f32[32,256]{1,0:T(8,128)} async-done(((f32[256,256]{1,0:T(8,128)}), f32[32,256]{1,0:T(8,128)}) %reduce-scatter.5.cloned.1.call-update) | async-done | bytes 32784 | tf_op jit(solution)/shard_map/reduce_scatter | solution.py:166
  (70 shorter events, 54.1 us)
Async XLA Ops:
  7.2 323.5 %reduce-scatter.3.cloned.1.call-start = ((), (), s32[]{:S(2)}) async-start(), calls=%async_computation.2 | async-start | bytes 1310720 | tf_op jit(solution)/shard_map/reduce_scatter | solution.py:165
  7.2 34.7 %copy-start.6 = (f32[32,16,1280]{2,1,0:T(8,128)S(1)}, f32[32,16,1280]{2,1,0:T(8,128)}, u32[]{:S(2)}) copy-start(f32[32,16,1280]{2,1,0:T(8,128)} %param.5) | copy-start | bytes 7864324
  9.8 32.1 %collective-permute-start = (f32[32,16,640]{2,1,0:T(8,128)}, f32[32,16,640]{2,1,0:T(8,128)}, u32[]{:S(2)}, u32[]{:S(2)}) collective-permute-start(f32[32,16,640]{2,1,0:T(8,128)} %constant_dynamic-slice_fusion.1), channel_id=1, source_target_pairs={{0,4},{4,0},{8,12},{12,8},{16,20},{20,16},{24,28},{28,24},{1,5},{5... | collective-permute-start | bytes 3932168 | tf_op jit(solution)/shard_map/ppermute | solution.py:139
  43.6 4.9 %collective-permute-start.2 = (f32[64,8,640]{2,1,0:T(8,128)S(1)}, f32[64,8,640]{2,1,0:T(8,128)S(1)}, u32[]{:S(2)}, u32[]{:S(2)}) collective-permute-start(f32[64,8,640]{2,1,0:T(8,128)S(1)} %get-tuple-element.22), channel_id=1, source_target_pairs={{1,0},{2,1},{3,2},{5,4},{6,5},{7,6},{9,8},{10,9},{11,10},{13,12},{... | collective-permute-start | bytes 3932168 | tf_op jit(solution)/shard_map/ppermute | solution.py:107
  44.9 5.7 %collective-permute-start.1 = (f32[64,8,640]{2,1,0:T(8,128)S(1)}, f32[64,8,640]{2,1,0:T(8,128)S(1)}, u32[]{:S(2)}, u32[]{:S(2)}) collective-permute-start(f32[64,8,640]{2,1,0:T(8,128)S(1)} %get-tuple-element.23), channel_id=1, source_target_pairs={{0,1},{1,2},{2,3},{4,5},{5,6},{6,7},{8,9},{9,10},{10,11},{12,13},{... | collective-permute-start | bytes 3932168 | tf_op jit(solution)/shard_map/ppermute | solution.py:106
  55.5 12.0 %collective-permute-start.4 = (f32[15,16,640]{2,1,0:T(8,128)S(1)}, f32[15,16,640]{2,1,0:T(8,128)S(1)}, u32[]{:S(2)}, u32[]{:S(2)}) collective-permute-start(f32[15,16,640]{2,1,0:T(8,128)S(1)} %get-tuple-element.20), channel_id=1, source_target_pairs={{8,0},{12,4},{16,8},{20,12},{24,16},{28,20},{9,1},{13,5},{17,9},{2... | collective-permute-start | bytes 1843208 | tf_op jit(solution)/shard_map/ppermute | solution.py:107
  56.8 12.2 %collective-permute-start.3 = (f32[15,16,640]{2,1,0:T(8,128)S(1)}, f32[15,16,640]{2,1,0:T(8,128)S(1)}, u32[]{:S(2)}, u32[]{:S(2)}) collective-permute-start(f32[15,16,640]{2,1,0:T(8,128)S(1)} %get-tuple-element.21), channel_id=1, source_target_pairs={{0,8},{4,12},{8,16},{12,20},{16,24},{20,28},{1,9},{5,13},{9,17},{1... | collective-permute-start | bytes 1843208 | tf_op jit(solution)/shard_map/ppermute | solution.py:106
  77.3 12.5 %collective-permute-start.6 = (f32[15,16,640]{2,1,0:T(8,128)S(1)}, f32[15,16,640]{2,1,0:T(8,128)S(1)}, u32[]{:S(2)}, u32[]{:S(2)}) collective-permute-start(f32[15,16,640]{2,1,0:T(8,128)S(1)} %get-tuple-element.18), channel_id=1, source_target_pairs={{8,0},{12,4},{16,8},{20,12},{24,16},{28,20},{9,1},{13,5},{17,9},{2... | collective-permute-start | bytes 1843208 | tf_op jit(solution)/shard_map/ppermute | solution.py:107
  78.6 12.7 %collective-permute-start.5 = (f32[15,16,640]{2,1,0:T(8,128)S(1)}, f32[15,16,640]{2,1,0:T(8,128)S(1)}, u32[]{:S(2)}, u32[]{:S(2)}) collective-permute-start(f32[15,16,640]{2,1,0:T(8,128)S(1)} %get-tuple-element.19), channel_id=1, source_target_pairs={{0,8},{4,12},{8,16},{12,20},{16,24},{20,28},{1,9},{5,13},{9,17},{1... | collective-permute-start | bytes 1843208 | tf_op jit(solution)/shard_map/ppermute | solution.py:106
  99.0 15.4 %collective-permute-start.8 = (f32[64,8,640]{2,1,0:T(8,128)S(1)}, f32[64,8,640]{2,1,0:T(8,128)S(1)}, u32[]{:S(2)}, u32[]{:S(2)}) collective-permute-start(f32[64,8,640]{2,1,0:T(8,128)S(1)} %get-tuple-element.16), channel_id=1, source_target_pairs={{1,0},{2,1},{3,2},{5,4},{6,5},{7,6},{9,8},{10,9},{11,10},{13,12},{... | collective-permute-start | bytes 3932168 | tf_op jit(solution)/shard_map/ppermute | solution.py:107
  100.3 16.1 %collective-permute-start.7 = (f32[64,8,640]{2,1,0:T(8,128)S(1)}, f32[64,8,640]{2,1,0:T(8,128)S(1)}, u32[]{:S(2)}, u32[]{:S(2)}) collective-permute-start(f32[64,8,640]{2,1,0:T(8,128)S(1)} %get-tuple-element.17), channel_id=1, source_target_pairs={{0,1},{1,2},{2,3},{4,5},{5,6},{6,7},{8,9},{9,10},{10,11},{12,13},{... | collective-permute-start | bytes 3932168 | tf_op jit(solution)/shard_map/ppermute | solution.py:106
  121.8 21.2 %collective-permute-start.10 = (f32[64,8,640]{2,1,0:T(8,128)S(1)}, f32[64,8,640]{2,1,0:T(8,128)S(1)}, u32[]{:S(2)}, u32[]{:S(2)}) collective-permute-start(f32[64,8,640]{2,1,0:T(8,128)S(1)} %get-tuple-element.14), channel_id=1, source_target_pairs={{1,0},{2,1},{3,2},{5,4},{6,5},{7,6},{9,8},{10,9},{11,10},{13,12},{... | collective-permute-start | bytes 3932168 | tf_op jit(solution)/shard_map/ppermute | solution.py:107
  123.1 21.9 %collective-permute-start.9 = (f32[64,8,640]{2,1,0:T(8,128)S(1)}, f32[64,8,640]{2,1,0:T(8,128)S(1)}, u32[]{:S(2)}, u32[]{:S(2)}) collective-permute-start(f32[64,8,640]{2,1,0:T(8,128)S(1)} %get-tuple-element.15), channel_id=1, source_target_pairs={{0,1},{1,2},{2,3},{4,5},{5,6},{6,7},{8,9},{9,10},{10,11},{12,13},{... | collective-permute-start | bytes 3932168 | tf_op jit(solution)/shard_map/ppermute | solution.py:106
  149.9 12.5 %collective-permute-start.12 = (f32[15,16,640]{2,1,0:T(8,128)S(1)}, f32[15,16,640]{2,1,0:T(8,128)S(1)}, u32[]{:S(2)}, u32[]{:S(2)}) collective-permute-start(f32[15,16,640]{2,1,0:T(8,128)S(1)} %get-tuple-element.12), channel_id=1, source_target_pairs={{8,0},{12,4},{16,8},{20,12},{24,16},{28,20},{9,1},{13,5},{17,9},{2... | collective-permute-start | bytes 1843208 | tf_op jit(solution)/shard_map/ppermute | solution.py:107
  151.2 12.7 %collective-permute-start.11 = (f32[15,16,640]{2,1,0:T(8,128)S(1)}, f32[15,16,640]{2,1,0:T(8,128)S(1)}, u32[]{:S(2)}, u32[]{:S(2)}) collective-permute-start(f32[15,16,640]{2,1,0:T(8,128)S(1)} %get-tuple-element.13), channel_id=1, source_target_pairs={{0,8},{4,12},{8,16},{12,20},{16,24},{20,28},{1,9},{5,13},{9,17},{1... | collective-permute-start | bytes 1843208 | tf_op jit(solution)/shard_map/ppermute | solution.py:106
  172.2 12.5 %collective-permute-start.14 = (f32[15,16,640]{2,1,0:T(8,128)S(1)}, f32[15,16,640]{2,1,0:T(8,128)S(1)}, u32[]{:S(2)}, u32[]{:S(2)}) collective-permute-start(f32[15,16,640]{2,1,0:T(8,128)S(1)} %get-tuple-element.10), channel_id=1, source_target_pairs={{8,0},{12,4},{16,8},{20,12},{24,16},{28,20},{9,1},{13,5},{17,9},{2... | collective-permute-start | bytes 1843208 | tf_op jit(solution)/shard_map/ppermute | solution.py:107
  173.5 12.7 %collective-permute-start.13 = (f32[15,16,640]{2,1,0:T(8,128)S(1)}, f32[15,16,640]{2,1,0:T(8,128)S(1)}, u32[]{:S(2)}, u32[]{:S(2)}) collective-permute-start(f32[15,16,640]{2,1,0:T(8,128)S(1)} %get-tuple-element.11), channel_id=1, source_target_pairs={{0,8},{4,12},{8,16},{12,20},{16,24},{20,28},{1,9},{5,13},{9,17},{1... | collective-permute-start | bytes 1843208 | tf_op jit(solution)/shard_map/ppermute | solution.py:106
  196.1 17.3 %collective-permute-start.16 = (f32[64,8,640]{2,1,0:T(8,128)}, f32[64,8,640]{2,1,0:T(8,128)}, u32[]{:S(2)}, u32[]{:S(2)}) collective-permute-start(f32[64,8,640]{2,1,0:T(8,128)} %get-tuple-element.8), channel_id=1, source_target_pairs={{1,0},{2,1},{3,2},{5,4},{6,5},{7,6},{9,8},{10,9},{11,10},{13,12},{... | collective-permute-start | bytes 3932168 | tf_op jit(solution)/shard_map/ppermute | solution.py:107
  197.4 17.9 %collective-permute-start.15 = (f32[64,8,640]{2,1,0:T(8,128)}, f32[64,8,640]{2,1,0:T(8,128)}, u32[]{:S(2)}, u32[]{:S(2)}) collective-permute-start(f32[64,8,640]{2,1,0:T(8,128)} %get-tuple-element.9), channel_id=1, source_target_pairs={{0,1},{1,2},{2,3},{4,5},{5,6},{6,7},{8,9},{9,10},{10,11},{12,13},{... | collective-permute-start | bytes 3932168 | tf_op jit(solution)/shard_map/ppermute | solution.py:106
  224.2 17.6 %collective-permute-start.17 = (f32[32,16,640]{2,1,0:T(8,128)S(1)}, f32[32,16,640]{2,1,0:T(8,128)S(1)}, u32[]{:S(2)}, u32[]{:S(2)}) collective-permute-start(f32[32,16,640]{2,1,0:T(8,128)S(1)} %constant_dynamic-slice_fusion), channel_id=1, source_target_pairs={{0,4},{4,0},{8,12},{12,8},{16,20},{20,16},{24,28},{28,24},{1,5},{5... | collective-permute-start | bytes 3932168 | tf_op jit(solution)/shard_map/ppermute | solution.py:148
  243.8 86.9 %copy-start.5 = (f32[32,16,1280]{2,1,0:T(8,128)}, f32[32,16,1280]{2,1,0:T(8,128)S(1)}, u32[]{:S(2)}) copy-start(f32[32,16,1280]{2,1,0:T(8,128)S(1)} %get-tuple-element.3) | copy-start | bytes 7864324
  305.3 90.3 %reduce-scatter.5.cloned.1.call-start = ((), (), s32[]{:S(2)}) async-start(), calls=%async_computation.3 | async-start | bytes 294912 | tf_op jit(solution)/shard_map/reduce_scatter | solution.py:166
  330.7 64.9 %copy-start.7 = (s32[256]{0:T(256)S(1)}, s32[256]{0:T(256)}, u32[]{:S(2)}) copy-start(s32[256]{0:T(256)} %param.9) | copy-start | bytes 3076
  330.7 64.9 %copy-start.8 = (s32[32]{0:T(128)S(1)}, s32[32]{0:T(128)}, u32[]{:S(2)}) copy-start(s32[32]{0:T(128)} %param.8) | copy-start | bytes 388
  (5 other events, 24.9 us)
Sparse Core Ops, SparseCore 0:
  305.4 25.2 reduce-scatter.2
  334.4 61.2 reduce-scatter.4

commit v2 on v1

--- a/solution.py
+++ b/solution.py
@@ -108,6 +108,148 @@
     return before, after
 
 
+def partner(axis, bit):
+    return lax.bitwise_xor(lax.axis_index(axis), bit)
+
+
+def bits_of(size):
+    return [1 << n for n in range(size.bit_length() - 1)]
+
+
+def greet(stages):
+    barrier = pltpu.get_barrier_semaphore()
+    for axis, bit in stages:
+        pl.semaphore_signal(
+            barrier,
+            inc=1,
+            device_id={axis: partner(axis, bit)},
+            device_id_type=pl.DeviceIdType.MESH,
+        )
+    pl.semaphore_wait(barrier, len(stages))
+
+
+def exchange(src, dst, send_sem, recv_sem, stage):
+    axis, bit = stage
+    copy = pltpu.make_async_remote_copy(
+        src_ref=src,
+        dst_ref=dst,
+        send_sem=send_sem,
+        recv_sem=recv_sem,
+        device_id={axis: partner(axis, bit)},
+        device_id_type=pl.DeviceIdType.MESH,
+    )
+    copy.start()
+    return copy
+
+
+def correlate_body(stages, groups, cells, est_ref, prow_ref, fcol_ref, out_ref, *scratch):
+    count = len(stages)
+    sums, got, sum_send, sum_recv, send_sem, recv_sem = scratch[:6]
+    held = scratch[6 : 6 + count]
+    landed = scratch[6 + count :]
+    mobs, rows_of = groups
+    prec = est_ref.shape[1] - mobs * out_ref.shape[1]
+    rows, columns = out_ref.shape
+    greet(stages)
+    sums[0] = jnp.broadcast_to(
+        jnp.sum(est_ref[...], axis=0, keepdims=True), sums.shape[1:]
+    )
+    for n, stage in enumerate(stages):
+        copy = exchange(sums.at[n], got.at[n], sum_send.at[n], sum_recv.at[n], stage)
+        copy.wait()
+        sums[n + 1] = sums[n] + got[n]
+    mean = sums[count, :1, :] / cells
+    left = (est_ref[:, :prec] - mean[:, :prec]).astype(jnp.bfloat16)
+    wide = left.astype(jnp.float32)
+    left_squares = jnp.sum(wide * wide, axis=0, keepdims=True)
+    across = left.T
+    first = held[0]
+    for m in range(mobs):
+        start = prec + m * columns
+        right = (
+            est_ref[:, start : start + columns] - mean[:, start : start + columns]
+        ).astype(jnp.bfloat16)
+        wide = right.astype(jnp.float32)
+        right_squares = jnp.sum(wide * wide, axis=0, keepdims=True)
+        product = jnp.dot(across, right, preferred_element_type=jnp.float32)
+        for r in range(rows_of):
+            block = first.at[m // 2, m % 2, r]
+            block[:rows, :] = product[r * rows : (r + 1) * rows, :]
+            block[rows : rows + 8, :] = jnp.broadcast_to(right_squares, (8, columns))
+            block[rows + 8 :, :] = jnp.broadcast_to(left_squares, (8, prec))
+    for n, stage in enumerate(stages):
+        axis, bit = stage
+        mine = lax.rem(lax.axis_index(axis) // bit, 2)
+        copy = exchange(
+            held[n].at[:, 1 - mine], landed[n], send_sem.at[n], recv_sem.at[n], stage
+        )
+        copy.wait()
+        span = held[n].shape[0]
+        for i in range(span):
+            total = held[n][i, mine] + landed[n][i]
+            if n + 1 == count:
+                column = 1.0 / jnp.sqrt(total[rows : rows + 1, :] + 1e-06)
+                row = 1.0 / jnp.sqrt(total[rows + 8 : rows + 9, :] + 1e-06)
+                place = lax.broadcasted_iota(jnp.int32, (rows, prec), 1)
+                wanted = lax.broadcasted_iota(jnp.int32, (rows, prec), 0)
+                wanted = wanted + lax.axis_index("rt") * rows
+                row = jnp.sum(jnp.where(place == wanted, row, 0.0), axis=1, keepdims=True)
+                same = (prow_ref[...] == fcol_ref[...]).astype(jnp.float32)
+                out_ref[...] = same * total[:rows, :] * row * column
+            elif stages[n + 1][0] == axis:
+                held[n + 1][i // 2, i % 2] = total
+            else:
+                for r in range(rows_of):
+                    held[n + 1][r // 2, r % 2] = total[r]
+
+
+def correlate(estimate, prec_window, frag_window):
+    frames, scans, channels = estimate.shape
+    mobs, rows_of = lax.axis_size("mob"), lax.axis_size("rt")
+    rows, columns = prec_window.shape[0], frag_window.shape[0]
+    stages = [("mob", bit) for bit in bits_of(mobs)] + [("rt", bit) for bit in bits_of(rows_of)]
+    count = len(stages)
+    tile = (rows + 16, columns)
+    held, landed = [], []
+    for axis, bit in stages:
+        if axis == "mob":
+            span, tail = mobs // (2 * bit), (rows_of,) + tile
+        else:
+            span, tail = rows_of // (2 * bit), tile
+        held.append(pltpu.VMEM((span, 2) + tail, jnp.float32))
+        landed.append(pltpu.VMEM((span,) + tail, jnp.float32))
+    whole = pl.BlockSpec(memory_space=pltpu.VMEM)
+    cells = frames * scans * mobs * rows_of
+    return pl.pallas_call(
+        functools.partial(correlate_body, stages, (mobs, rows_of), cells),
+        in_specs=[whole] * 3,
+        out_specs=whole,
+        out_shape=jax.ShapeDtypeStruct((rows, columns), jnp.float32),
+        scratch_shapes=[
+            pltpu.VMEM((count + 1, SUB, channels), jnp.float32),
+            pltpu.VMEM((count, SUB, channels), jnp.float32),
+            pltpu.SemaphoreType.DMA((count,)),
+            pltpu.SemaphoreType.DMA((count,)),
+            pltpu.SemaphoreType.DMA((count,)),
+            pltpu.SemaphoreType.DMA((count,)),
+        ]
+        + held
+        + landed,
+        compiler_params=pltpu.CompilerParams(
+            collective_id=1, has_side_effects=True, vmem_limit_bytes=40 * 1024 * 1024
+        ),
+        cost_estimate=pl.CostEstimate(
+            flops=2 * frames * scans * PREC * (channels - PREC),
+            bytes_accessed=4 * frames * scans * channels,
+            transcendentals=0,
+        ),
+    )(
+        estimate.reshape(frames * scans, channels),
+        prec_window.reshape(rows, 1),
+        frag_window.reshape(1, columns),
+    )
+
+
 def local(observed, frame_kernel, scan_kernel, prec_window, frag_window):
     frames, scan_count, channels = observed.shape
     radius = (frame_kernel.shape[0] - 1) // 2
@@ -149,33 +291,7 @@
     estimate = jnp.concatenate(
         [jnp.where(first, mine, other), jnp.where(first, other, mine)], axis=2
     )
-    profiles = estimate.reshape(frames * scan_count, channels)
-    cell_count = frames * scan_count * lax.axis_size("rt") * lax.axis_size("mob")
-    channel_total = lax.psum(jnp.sum(profiles, axis=0), ("rt", "mob"))
-    channel_mean = channel_total / cell_count
-    centered = (profiles - channel_mean).astype(jnp.bfloat16)
-    as_float = centered.astype(jnp.float32)
-    squares = lax.psum(jnp.sum(as_float * as_float, axis=0), ("rt", "mob"))
-    cross_sums = lax.dot_general(
-        centered[:, :PREC],
-        centered[:, PREC:],
-        (((0,), (0,)), ((), ())),
-        preferred_element_type=jnp.float32,
-    )
-    partial_value = lax.psum_scatter(cross_sums, "mob", scatter_dimension=1, tiled=True)
-    block_sums = lax.psum_scatter(partial_value, "rt", scatter_dimension=0, tiled=True)
-    row_count = prec_window.shape[0]
-    column_count = frag_window.shape[0]
-    inverse_norm = 1.0 / jnp.sqrt(squares + 1e-06)
-    row_inverse = lax.dynamic_slice_in_dim(
-        inverse_norm[:PREC], lax.axis_index("rt") * row_count, row_count
-    )
-    column_inverse = lax.dynamic_slice_in_dim(
-        inverse_norm[PREC:], lax.axis_index("mob") * column_count, column_count
-    )
-    pair_mask = (prec_window[:, None] == frag_window[None, :]).astype(jnp.float32)
-    correlation = pair_mask * block_sums * row_inverse[:, None] * column_inverse[None, :]
-    return (estimate, correlation)
+    return (estimate, correlate(estimate, prec_window, frag_window))
 
 
 def solution(mesh):

time: 405 us -> 306 us (0.76)
  blocking collectives: 99.4 us -> 0 us
  Pallas kernels: 52 us -> 107 us
  waiting for transfers between devices: 135 us -> 109 us
  between operations: 14.4 us -> 1.01 us
  starting transfers between devices: 86.7 us -> 74 us
    psum x2 -> x0, blocking collectives: 99.4 us -> none  [the longest x1 59.8 us: local(): channel_total = lax.psum(jnp.sum(profiles, axis=0), ('rt', 'mob'))]
    pallas_call x0 -> x1, Pallas kernels: none -> 54.9 us  [correlate(): pl.pallas_call(functools.partial(correlate_body, stages, (mobs, rows_of),...]
    reduce_scatter x2 -> x0, waiting for transfers between devices: 50.2 us -> none  [the longest x1 25.3 us: local(): lax.psum_scatter(cross_sums, 'mob', scatter_dimension=1, tiled=True)]
    ppermute x8, waiting for transfers between devices: 13.9 us -> 30.2 us  [halo(): lax.ppermute(lax.slice_in_dim(cells, size - width, size, axis=dim), axis,...]
    ppermute x8, starting transfers between devices: 71.8 us -> 59.2 us  [halo(): lax.ppermute(lax.slice_in_dim(cells, size - width, size, axis=dim), axis,...]
    ppermute x8, waiting for transfers between devices: 25.9 us -> 33.9 us  [halo(): lax.ppermute(lax.slice_in_dim(cells, 0, width, axis=dim), axis, down)]
  transfers between devices with their start and end apart: 20 -> 18, of which waited for: 19 -> 18; matrix products, arithmetic and copies ran while one was open for 0% -> 0% of each run, Pallas kernels for 0% -> 0%
where the time goes in v2:
time: 306 us; the launch traced here: 305 us
  waiting for transfers between devices  109 us (36%)
  Pallas kernels  107 us (35%)
  starting transfers between devices  74 us (24%)
  local copies, waits for them, and re-layouts  9.92 us (3%)
  other arithmetic  3.65 us (1%)
    ppermute x8, starting transfers between devices, halo(): lax.ppermute(lax.slice_in_dim(cells, size - width, size, axis=dim), axis,...  59.2 us
    pallas_call x1, Pallas kernels, correlate(): pl.pallas_call(functools.partial(correlate_body, stages, (mobs, rows_of),...  54.9 us
    pallas_call x8, Pallas kernels, blur(): pl.pallas_call(body, grid=(channels // LANES,), in_specs=[pl.BlockSpec(me...  52 us
    ppermute x2, waiting for transfers between devices, local(): other = lax.ppermute(other, 'rt', swap)  45.3 us
    ppermute x8, waiting for transfers between devices, halo(): lax.ppermute(lax.slice_in_dim(cells, 0, width, axis=dim), axis, down)  33.9 us
    ppermute x8, waiting for transfers between devices, halo(): lax.ppermute(lax.slice_in_dim(cells, size - width, size, axis=dim), axis,...  30.2 us
    ppermute x8, starting transfers between devices, halo(): lax.ppermute(lax.slice_in_dim(cells, 0, width, axis=dim), axis, down)  10.3 us
  transfers between devices with their start and end apart: 18, of which 18 were waited for; matrix products, arithmetic and copies ran while one was open for 0% of the time, Pallas kernels for 0%

profile of v2, /device:TPU:0, one launch (start us, length us, event | category | flops | bytes accessed | tf_op | source)
XLA Modules:
  0.0 305.0 jit_solution(3650181473042790562)
XLA Ops:
  6.2 29.1 %collective-permute-done = f32[32,16,640]{2,1,0:T(8,128)} collective-permute-done((f32[32,16,640]{2,1,0:T(8,128)}, f32[32,16,640]{2,1,0:T(8,128)}, u32[]{:S(2)}, u32[]{:S(2)}) %collective-permute-start) | collective-permute-done | bytes 1310752 | tf_op jit(solution)/shard_map/ppermute | solution.py:281
  41.0 4.2 %collective-permute-done.2.hi_ref = f32[64,8,640]{2,1,0:T(8,128)S(1)} collective-permute-done((f32[64,8,640]{2,1,0:T(8,128)S(1)}, f32[64,8,640]{2,1,0:T(8,128)S(1)}, u32[]{:S(2)}, u32[]{:S(2)}) %collective-permute-start.2) | collective-permute-done | bytes 1310752 | tf_op jit(solution)/shard_map/ppermute | solution.py:107
  45.2 4.8 %shard_map.68.mid_ref = f32[64,16,640]{2,1,0:T(8,128)S(1)} custom-call(f32[15]{0:T(128)S(1)} %copy-done.5, f32[64,16,640]{2,1,0:T(8,128)S(1)} %pad_maximum_fusion.mid_ref.rest_0_, f32[64,8,640]{2,1,0:T(8,128)S(1)} %collective-permute-done.1.lo_ref, f32[64,8,640]{2,1,0:T(8,128)S(1)} %collective-permute-done.2.hi_ref), custom_call_target="tpu_custom_call" | custom-call | flops 19660800 | bytes 7864320 | tf_op jit(solution)/shard_map/pallas_call | solution.py:85
  55.0 6.3 %collective-permute-done.3.lo_ref = f32[15,16,640]{2,1,0:T(8,128)S(1)} collective-permute-done((f32[15,16,640]{2,1,0:T(8,128)S(1)}, f32[15,16,640]{2,1,0:T(8,128)S(1)}, u32[]{:S(2)}, u32[]{:S(2)}) %collective-permute-start.3) | collective-permute-done | bytes 614432 | tf_op jit(solution)/shard_map/ppermute | solution.py:106
  61.3 4.4 %collective-permute-done.4.hi_ref = f32[15,16,640]{2,1,0:T(8,128)S(1)} collective-permute-done((f32[15,16,640]{2,1,0:T(8,128)S(1)}, f32[15,16,640]{2,1,0:T(8,128)S(1)}, u32[]{:S(2)}, u32[]{:S(2)}) %collective-permute-start.4) | collective-permute-done | bytes 614432 | tf_op jit(solution)/shard_map/ppermute | solution.py:107
  65.7 8.2 %shard_map.69.mid_ref = f32[64,16,640]{2,1,0:T(8,128)S(1)} custom-call(f32[31]{0:T(128)S(1)} %copy-done.4, f32[64,16,640]{2,1,0:T(8,128)S(1)} %shard_map.68.mid_ref, f32[15,16,640]{2,1,0:T(8,128)S(1)} %collective-permute-done.3.lo_ref, f32[15,16,640]{2,1,0:T(8,128)S(1)} %collective-permute-done.4.hi_ref, f32[64,16,640]{2,1,0:T(8,128)S(1)} %pad_maximum_fusion.mid_ref.rest_0_), custom_call_target="tpu_custom_call" | custom-call | flops 40632320 | bytes 7864320 | tf_op jit(solution)/shard_map/pallas_call | solution.py:85
  78.8 6.3 %collective-permute-done.5.lo_ref = f32[15,16,640]{2,1,0:T(8,128)S(1)} collective-permute-done((f32[15,16,640]{2,1,0:T(8,128)S(1)}, f32[15,16,640]{2,1,0:T(8,128)S(1)}, u32[]{:S(2)}, u32[]{:S(2)}) %collective-permute-start.5) | collective-permute-done | bytes 614432 | tf_op jit(solution)/shard_map/ppermute | solution.py:106
  85.1 4.4 %collective-permute-done.6.hi_ref = f32[15,16,640]{2,1,0:T(8,128)S(1)} collective-permute-done((f32[15,16,640]{2,1,0:T(8,128)S(1)}, f32[15,16,640]{2,1,0:T(8,128)S(1)}, u32[]{:S(2)}, u32[]{:S(2)}) %collective-permute-start.6) | collective-permute-done | bytes 614432 | tf_op jit(solution)/shard_map/ppermute | solution.py:107
  89.5 7.6 %shard_map.70.mid_ref = f32[64,16,640]{2,1,0:T(8,128)S(1)} custom-call(f32[31]{0:T(128)S(1)} %copy-done.4, f32[64,16,640]{2,1,0:T(8,128)S(1)} %shard_map.69.mid_ref, f32[15,16,640]{2,1,0:T(8,128)S(1)} %collective-permute-done.5.lo_ref, f32[15,16,640]{2,1,0:T(8,128)S(1)} %collective-permute-done.6.hi_ref), custom_call_target="tpu_custom_call" | custom-call | flops 40632320 | bytes 7864320 | tf_op jit(solution)/shard_map/pallas_call | solution.py:85
  97.3 13.9 %collective-permute-start.7 = (f32[64,8,640]{2,1,0:T(8,128)S(1)}, f32[64,8,640]{2,1,0:T(8,128)S(1)}, u32[]{:S(2)}, u32[]{:S(2)}) collective-permute-start(f32[64,8,640]{2,1,0:T(8,128)S(1)} %get-tuple-element.15), channel_id=1, source_target_pairs={{0,1},{1,2},{2,3},{4,5},{5,6},{6,7},{8,9},{9,10},{10,11},{12,13},{... | collective-permute-start | bytes 3932168 | tf_op jit(solution)/shard_map/ppermute | solution.py:106
  118.0 5.2 %shard_map.71.mid_ref.rest_0_ = f32[64,16,640]{2,1,0:T(8,128)S(1)} custom-call(f32[15]{0:T(128)S(1)} %copy-done.5, f32[64,16,640]{2,1,0:T(8,128)S(1)} %shard_map.70.mid_ref, f32[64,8,640]{2,1,0:T(8,128)S(1)} %collective-permute-done.7.lo_ref, f32[64,8,640]{2,1,0:T(8,128)S(1)} %collective-permute-done.8.hi_ref, f32[64,16,640]{2,1,0:T(8,128)S(1)} %pad_maximum_fusion.mid_ref.rest_0_), custom_call_target="tpu_custom_call" | custom-call | flops 19660800 | bytes 7864320 | tf_op jit(solution)/shard_map/pallas_call | solution.py:85
  124.6 17.1 %collective-permute-start.9 = (f32[64,8,640]{2,1,0:T(8,128)S(1)}, f32[64,8,640]{2,1,0:T(8,128)S(1)}, u32[]{:S(2)}, u32[]{:S(2)}) collective-permute-start(f32[64,8,640]{2,1,0:T(8,128)S(1)} %get-tuple-element.13), channel_id=1, source_target_pairs={{0,1},{1,2},{2,3},{4,5},{5,6},{6,7},{8,9},{9,10},{10,11},{12,13},{... | collective-permute-start | bytes 3932168 | tf_op jit(solution)/shard_map/ppermute | solution.py:106
  144.3 4.8 %shard_map.72.mid_ref = f32[64,16,640]{2,1,0:T(8,128)S(1)} custom-call(f32[15]{0:T(128)S(1)} %copy-done.5, f32[64,16,640]{2,1,0:T(8,128)S(1)} %shard_map.71.mid_ref.rest_0_, f32[64,8,640]{2,1,0:T(8,128)S(1)} %collective-permute-done.9.lo_ref, f32[64,8,640]{2,1,0:T(8,128)S(1)} %collective-permute-done.10.hi_ref), custom_call_target="tpu_custom_call" | custom-call | flops 19660800 | bytes 7864320 | tf_op jit(solution)/shard_map/pallas_call | solution.py:85
  154.4 6.3 %collective-permute-done.11.lo_ref = f32[15,16,640]{2,1,0:T(8,128)S(1)} collective-permute-done((f32[15,16,640]{2,1,0:T(8,128)S(1)}, f32[15,16,640]{2,1,0:T(8,128)S(1)}, u32[]{:S(2)}, u32[]{:S(2)}) %collective-permute-start.11) | collective-permute-done | bytes 614432 | tf_op jit(solution)/shard_map/ppermute | solution.py:106
  160.7 4.4 %collective-permute-done.12.hi_ref = f32[15,16,640]{2,1,0:T(8,128)S(1)} collective-permute-done((f32[15,16,640]{2,1,0:T(8,128)S(1)}, f32[15,16,640]{2,1,0:T(8,128)S(1)}, u32[]{:S(2)}, u32[]{:S(2)}) %collective-permute-start.12) | collective-permute-done | bytes 614432 | tf_op jit(solution)/shard_map/ppermute | solution.py:107
  165.1 8.2 %shard_map.73.mid_ref = f32[64,16,640]{2,1,0:T(8,128)S(1)} custom-call(f32[31]{0:T(128)S(1)} %copy-done.4, f32[64,16,640]{2,1,0:T(8,128)S(1)} %shard_map.72.mid_ref, f32[15,16,640]{2,1,0:T(8,128)S(1)} %collective-permute-done.11.lo_ref, f32[15,16,640]{2,1,0:T(8,128)S(1)} %collective-permute-done.12.hi_ref, f32[64,16,640]{2,1,0:T(8,128)S(1)} %pad_maximum_fusion.mid_ref.rest_0_), custom_call_target="tpu_custom_call" | custom-call | flops 40632320 | bytes 7864320 | tf_op jit(solution)/shard_map/pallas_call | solution.py:85
  176.6 6.3 %collective-permute-done.13.lo_ref = f32[15,16,640]{2,1,0:T(8,128)S(1)} collective-permute-done((f32[15,16,640]{2,1,0:T(8,128)S(1)}, f32[15,16,640]{2,1,0:T(8,128)S(1)}, u32[]{:S(2)}, u32[]{:S(2)}) %collective-permute-start.13) | collective-permute-done | bytes 614432 | tf_op jit(solution)/shard_map/ppermute | solution.py:106
  182.9 4.4 %collective-permute-done.14.hi_ref = f32[15,16,640]{2,1,0:T(8,128)S(1)} collective-permute-done((f32[15,16,640]{2,1,0:T(8,128)S(1)}, f32[15,16,640]{2,1,0:T(8,128)S(1)}, u32[]{:S(2)}, u32[]{:S(2)}) %collective-permute-start.14) | collective-permute-done | bytes 614432 | tf_op jit(solution)/shard_map/ppermute | solution.py:107
  187.3 7.6 %shard_map.74.mid_ref = f32[64,16,640]{2,1,0:T(8,128)S(1)} custom-call(f32[31]{0:T(128)S(1)} %copy-done.4, f32[64,16,640]{2,1,0:T(8,128)S(1)} %shard_map.73.mid_ref, f32[15,16,640]{2,1,0:T(8,128)S(1)} %collective-permute-done.13.lo_ref, f32[15,16,640]{2,1,0:T(8,128)S(1)} %collective-permute-done.14.hi_ref), custom_call_target="tpu_custom_call" | custom-call | flops 40632320 | bytes 7864320 | tf_op jit(solution)/shard_map/pallas_call | solution.py:85
  197.3 14.0 %collective-permute-start.15 = (f32[64,8,640]{2,1,0:T(8,128)}, f32[64,8,640]{2,1,0:T(8,128)}, u32[]{:S(2)}, u32[]{:S(2)}) collective-permute-start(f32[64,8,640]{2,1,0:T(8,128)} %get-tuple-element.7), channel_id=1, source_target_pairs={{0,1},{1,2},{2,3},{4,5},{5,6},{6,7},{8,9},{9,10},{10,11},{12,13},{... | collective-permute-start | bytes 3932168 | tf_op jit(solution)/shard_map/ppermute | solution.py:106
  213.2 7.2 %collective-permute-done.16.hi_ref = f32[64,8,640]{2,1,0:T(8,128)} collective-permute-done((f32[64,8,640]{2,1,0:T(8,128)}, f32[64,8,640]{2,1,0:T(8,128)}, u32[]{:S(2)}, u32[]{:S(2)}) %collective-permute-start.16) | collective-permute-done | bytes 1310752 | tf_op jit(solution)/shard_map/ppermute | solution.py:107
  222.2 5.7 %shard_map.75 = f32[64,16,640]{2,1,0:T(8,128)S(1)} custom-call(f32[15]{0:T(128)S(1)} %copy-done.5, f32[64,16,640]{2,1,0:T(8,128)S(1)} %copy-done.1, f32[64,8,640]{2,1,0:T(8,128)} %collective-permute-done.15.lo_ref, f32[64,8,640]{2,1,0:T(8,128)} %collective-permute-done.16.hi_ref, f32[64,16,640]{2,1,0:T(8,128)S(1)} %shard_map.71.mid_ref.rest_0_), custom_call_target="tpu_custom_call" | custom-call | flops 19660800 | bytes 7864320 | tf_op jit(solution)/shard_map/pallas_call | solution.py:85
  231.0 16.3 %collective-permute-done.17 = f32[32,16,640]{2,1,0:T(8,128)S(1)} collective-permute-done((f32[32,16,640]{2,1,0:T(8,128)S(1)}, f32[32,16,640]{2,1,0:T(8,128)S(1)}, u32[]{:S(2)}, u32[]{:S(2)}) %collective-permute-start.17) | collective-permute-done | bytes 1310752 | tf_op jit(solution)/shard_map/ppermute | solution.py:290
  249.5 54.9 %shard_map.76 = f32[32,256]{1,0:T(8,128)S(1)} custom-call(f32[512,1280]{1,0:T(8,128)S(1)} %bitcast.3, s32[32,1]{1,0:T(8,128)S(1)} %copy.7.prow_ref, s32[1,256]{1,0:T(1,128)S(1)} %bitcast.4), custom_call_target="tpu_custom_call" | custom-call | flops 268435456 | bytes 2621440 | tf_op jit(solution)/shard_map/pallas_call | solution.py:223
  (55 shorter events, 52.2 us)
Async XLA Ops:
  0.6 34.7 %copy-start.7 = (f32[32,16,1280]{2,1,0:T(8,128)S(1)}, f32[32,16,1280]{2,1,0:T(8,128)}, u32[]{:S(2)}) copy-start(f32[32,16,1280]{2,1,0:T(8,128)} %param.5) | copy-start | bytes 7864324
  3.3 32.1 %collective-permute-start = (f32[32,16,640]{2,1,0:T(8,128)}, f32[32,16,640]{2,1,0:T(8,128)}, u32[]{:S(2)}, u32[]{:S(2)}) collective-permute-start(f32[32,16,640]{2,1,0:T(8,128)} %constant_dynamic-slice_fusion.1), channel_id=1, source_target_pairs={{0,4},{4,0},{8,12},{12,8},{16,20},{20,16},{24,28},{28,24},{1,5},{5... | collective-permute-start | bytes 3932168 | tf_op jit(solution)/shard_map/ppermute | solution.py:281
  37.0 3.9 %collective-permute-start.1 = (f32[64,8,640]{2,1,0:T(8,128)S(1)}, f32[64,8,640]{2,1,0:T(8,128)S(1)}, u32[]{:S(2)}, u32[]{:S(2)}) collective-permute-start(f32[64,8,640]{2,1,0:T(8,128)S(1)} %get-tuple-element.21), channel_id=1, source_target_pairs={{0,1},{1,2},{2,3},{4,5},{5,6},{6,7},{8,9},{9,10},{10,11},{12,13},{... | collective-permute-start | bytes 3932168 | tf_op jit(solution)/shard_map/ppermute | solution.py:106
  38.4 6.8 %copy-start.5 = (f32[15]{0:T(128)S(1)}, f32[15]{0:T(128)}, u32[]{:S(2)}) copy-start(f32[15]{0:T(128)} %k_ref.15) | copy-start | bytes 184
  38.4 6.8 %collective-permute-start.2 = (f32[64,8,640]{2,1,0:T(8,128)S(1)}, f32[64,8,640]{2,1,0:T(8,128)S(1)}, u32[]{:S(2)}, u32[]{:S(2)}) collective-permute-start(f32[64,8,640]{2,1,0:T(8,128)S(1)} %get-tuple-element.20), channel_id=1, source_target_pairs={{1,0},{2,1},{3,2},{5,4},{6,5},{7,6},{9,8},{10,9},{11,10},{13,12},{... | collective-permute-start | bytes 3932168 | tf_op jit(solution)/shard_map/ppermute | solution.py:107
  50.0 15.7 %copy-start.4 = (f32[31]{0:T(128)S(1)}, f32[31]{0:T(128)}, u32[]{:S(2)}) copy-start(f32[31]{0:T(128)} %k_ref.14) | copy-start | bytes 376
  50.2 11.1 %collective-permute-start.3 = (f32[15,16,640]{2,1,0:T(8,128)S(1)}, f32[15,16,640]{2,1,0:T(8,128)S(1)}, u32[]{:S(2)}, u32[]{:S(2)}) collective-permute-start(f32[15,16,640]{2,1,0:T(8,128)S(1)} %get-tuple-element.19), channel_id=1, source_target_pairs={{0,8},{4,12},{8,16},{12,20},{16,24},{20,28},{1,9},{5,13},{9,17},{1... | collective-permute-start | bytes 1843208 | tf_op jit(solution)/shard_map/ppermute | solution.py:106
  53.7 12.0 %collective-permute-start.4 = (f32[15,16,640]{2,1,0:T(8,128)S(1)}, f32[15,16,640]{2,1,0:T(8,128)S(1)}, u32[]{:S(2)}, u32[]{:S(2)}) collective-permute-start(f32[15,16,640]{2,1,0:T(8,128)S(1)} %get-tuple-element.18), channel_id=1, source_target_pairs={{8,0},{12,4},{16,8},{20,12},{24,16},{28,20},{9,1},{13,5},{17,9},{2... | collective-permute-start | bytes 1843208 | tf_op jit(solution)/shard_map/ppermute | solution.py:107
  74.0 11.1 %collective-permute-start.5 = (f32[15,16,640]{2,1,0:T(8,128)S(1)}, f32[15,16,640]{2,1,0:T(8,128)S(1)}, u32[]{:S(2)}, u32[]{:S(2)}) collective-permute-start(f32[15,16,640]{2,1,0:T(8,128)S(1)} %get-tuple-element.17), channel_id=1, source_target_pairs={{0,8},{4,12},{8,16},{12,20},{16,24},{20,28},{1,9},{5,13},{9,17},{1... | collective-permute-start | bytes 1843208 | tf_op jit(solution)/shard_map/ppermute | solution.py:106
  77.5 12.0 %collective-permute-start.6 = (f32[15,16,640]{2,1,0:T(8,128)S(1)}, f32[15,16,640]{2,1,0:T(8,128)S(1)}, u32[]{:S(2)}, u32[]{:S(2)}) collective-permute-start(f32[15,16,640]{2,1,0:T(8,128)S(1)} %get-tuple-element.16), channel_id=1, source_target_pairs={{8,0},{12,4},{16,8},{20,12},{24,16},{28,20},{9,1},{13,5},{17,9},{2... | collective-permute-start | bytes 1843208 | tf_op jit(solution)/shard_map/ppermute | solution.py:107
  97.3 16.5 %collective-permute-start.7 = (f32[64,8,640]{2,1,0:T(8,128)S(1)}, f32[64,8,640]{2,1,0:T(8,128)S(1)}, u32[]{:S(2)}, u32[]{:S(2)}) collective-permute-start(f32[64,8,640]{2,1,0:T(8,128)S(1)} %get-tuple-element.15), channel_id=1, source_target_pairs={{0,1},{1,2},{2,3},{4,5},{5,6},{6,7},{8,9},{9,10},{10,11},{12,13},{... | collective-permute-start | bytes 3932168 | tf_op jit(solution)/shard_map/ppermute | solution.py:106
  111.2 6.8 %collective-permute-start.8 = (f32[64,8,640]{2,1,0:T(8,128)S(1)}, f32[64,8,640]{2,1,0:T(8,128)S(1)}, u32[]{:S(2)}, u32[]{:S(2)}) collective-permute-start(f32[64,8,640]{2,1,0:T(8,128)S(1)} %get-tuple-element.14), channel_id=1, source_target_pairs={{1,0},{2,1},{3,2},{5,4},{6,5},{7,6},{9,8},{10,9},{11,10},{13,12},{... | collective-permute-start | bytes 3932168 | tf_op jit(solution)/shard_map/ppermute | solution.py:107
  123.3 18.9 %collective-permute-start.10 = (f32[64,8,640]{2,1,0:T(8,128)S(1)}, f32[64,8,640]{2,1,0:T(8,128)S(1)}, u32[]{:S(2)}, u32[]{:S(2)}) collective-permute-start(f32[64,8,640]{2,1,0:T(8,128)S(1)} %get-tuple-element.12), channel_id=1, source_target_pairs={{1,0},{2,1},{3,2},{5,4},{6,5},{7,6},{9,8},{10,9},{11,10},{13,12},{... | collective-permute-start | bytes 3932168 | tf_op jit(solution)/shard_map/ppermute | solution.py:107
  124.6 19.7 %collective-permute-start.9 = (f32[64,8,640]{2,1,0:T(8,128)S(1)}, f32[64,8,640]{2,1,0:T(8,128)S(1)}, u32[]{:S(2)}, u32[]{:S(2)}) collective-permute-start(f32[64,8,640]{2,1,0:T(8,128)S(1)} %get-tuple-element.13), channel_id=1, source_target_pairs={{0,1},{1,2},{2,3},{4,5},{5,6},{6,7},{8,9},{9,10},{10,11},{12,13},{... | collective-permute-start | bytes 3932168 | tf_op jit(solution)/shard_map/ppermute | solution.py:106
  149.2 11.5 %collective-permute-start.11 = (f32[15,16,640]{2,1,0:T(8,128)S(1)}, f32[15,16,640]{2,1,0:T(8,128)S(1)}, u32[]{:S(2)}, u32[]{:S(2)}) collective-permute-start(f32[15,16,640]{2,1,0:T(8,128)S(1)} %get-tuple-element.11), channel_id=1, source_target_pairs={{0,8},{4,12},{8,16},{12,20},{16,24},{20,28},{1,9},{5,13},{9,17},{1... | collective-permute-start | bytes 1843208 | tf_op jit(solution)/shard_map/ppermute | solution.py:106
  153.1 12.0 %collective-permute-start.12 = (f32[15,16,640]{2,1,0:T(8,128)S(1)}, f32[15,16,640]{2,1,0:T(8,128)S(1)}, u32[]{:S(2)}, u32[]{:S(2)}) collective-permute-start(f32[15,16,640]{2,1,0:T(8,128)S(1)} %get-tuple-element.10), channel_id=1, source_target_pairs={{8,0},{12,4},{16,8},{20,12},{24,16},{28,20},{9,1},{13,5},{17,9},{2... | collective-permute-start | bytes 1843208 | tf_op jit(solution)/shard_map/ppermute | solution.py:107
  173.4 9.5 %collective-permute-start.13 = (f32[15,16,640]{2,1,0:T(8,128)S(1)}, f32[15,16,640]{2,1,0:T(8,128)S(1)}, u32[]{:S(2)}, u32[]{:S(2)}) collective-permute-start(f32[15,16,640]{2,1,0:T(8,128)S(1)} %get-tuple-element.9), channel_id=1, source_target_pairs={{0,8},{4,12},{8,16},{12,20},{16,24},{20,28},{1,9},{5,13},{9,17},{1... | collective-permute-start | bytes 1843208 | tf_op jit(solution)/shard_map/ppermute | solution.py:106
  175.3 12.0 %collective-permute-start.14 = (f32[15,16,640]{2,1,0:T(8,128)S(1)}, f32[15,16,640]{2,1,0:T(8,128)S(1)}, u32[]{:S(2)}, u32[]{:S(2)}) collective-permute-start(f32[15,16,640]{2,1,0:T(8,128)S(1)} %get-tuple-element.8), channel_id=1, source_target_pairs={{8,0},{12,4},{16,8},{20,12},{24,16},{28,20},{9,1},{13,5},{17,9},{2... | collective-permute-start | bytes 1843208 | tf_op jit(solution)/shard_map/ppermute | solution.py:107
  194.9 2.4 copy-start
  197.3 15.9 %collective-permute-start.15 = (f32[64,8,640]{2,1,0:T(8,128)}, f32[64,8,640]{2,1,0:T(8,128)}, u32[]{:S(2)}, u32[]{:S(2)}) collective-permute-start(f32[64,8,640]{2,1,0:T(8,128)} %get-tuple-element.7), channel_id=1, source_target_pairs={{0,1},{1,2},{2,3},{4,5},{5,6},{6,7},{8,9},{9,10},{10,11},{12,13},{... | collective-permute-start | bytes 3932168 | tf_op jit(solution)/shard_map/ppermute | solution.py:106
  211.3 9.1 %collective-permute-start.16 = (f32[64,8,640]{2,1,0:T(8,128)}, f32[64,8,640]{2,1,0:T(8,128)}, u32[]{:S(2)}, u32[]{:S(2)}) collective-permute-start(f32[64,8,640]{2,1,0:T(8,128)} %get-tuple-element.6), channel_id=1, source_target_pairs={{1,0},{2,1},{3,2},{5,4},{6,5},{7,6},{9,8},{10,9},{11,10},{13,12},{... | collective-permute-start | bytes 3932168 | tf_op jit(solution)/shard_map/ppermute | solution.py:107
  227.9 3.0 copy-start.8
  229.4 17.9 %collective-permute-start.17 = (f32[32,16,640]{2,1,0:T(8,128)S(1)}, f32[32,16,640]{2,1,0:T(8,128)S(1)}, u32[]{:S(2)}, u32[]{:S(2)}) collective-permute-start(f32[32,16,640]{2,1,0:T(8,128)S(1)} %constant_dynamic-slice_fusion), channel_id=1, source_target_pairs={{0,4},{4,0},{8,12},{12,8},{16,20},{20,16},{24,28},{28,24},{1,5},{5... | collective-permute-start | bytes 3932168 | tf_op jit(solution)/shard_map/ppermute | solution.py:290
  249.1 55.2 %copy-start.2 = (f32[32,16,1280]{2,1,0:T(8,128)}, f32[32,16,1280]{2,1,0:T(8,128)S(1)}, u32[]{:S(2)}) copy-start(f32[32,16,1280]{2,1,0:T(8,128)S(1)} %pad_maximum_fusion.1) | copy-start | bytes 7864324
  (3 other events, 3.9 us)

commit v3 on v2

--- a/solution.py
+++ b/solution.py
@@ -14,98 +14,325 @@
 STEP = 16
 
 
-def scan_taps(pad_ref, frame, taps, scans):
+def flipped(k_ref, flip):
+    count = k_ref.shape[0]
+    return [k_ref[count - 1 - a if flip else a] for a in range(count)]
+
+
+def blur_scans(taps, src, scans, emit):
     radius = (len(taps) - 1) // 2
-    total = None
-    for a, tap in enumerate(taps):
-        part = tap * pad_ref[frame, pl.ds(SUB - radius + a, scans), :]
-        total = part if total is None else total + part
-    return total
-
-
-def scan_kernel_body(flip, k_ref, mid_ref, lo_ref, hi_ref, *rest):
-    *scale, out_ref, pad_ref = rest
-    frames, scans, _ = mid_ref.shape
-    count = k_ref.shape[0]
-    taps = [k_ref[count - 1 - a if flip else a] for a in range(count)]
-    pad_ref[:, :SUB, :] = lo_ref[...]
-    pad_ref[:, SUB : SUB + scans, :] = mid_ref[...]
-    pad_ref[:, SUB + scans :, :] = hi_ref[...]
 
     def one(frame, carry):
-        total = scan_taps(pad_ref, frame, taps, scans)
-        if scale:
-            total = scale[0][frame] * total
-        out_ref[frame] = total
-        return carry
-
-    lax.fori_loop(0, frames, one, 0, unroll=4)
-
-
-def frame_kernel_body(flip, divide, k_ref, mid_ref, lo_ref, hi_ref, *rest):
-    *above, out_ref, pad_ref = rest
-    frames, scans, _ = mid_ref.shape
-    count = k_ref.shape[0]
-    radius = (count - 1) // 2
-    pad_ref[:radius] = lo_ref[...]
-    pad_ref[radius : radius + frames] = mid_ref[...]
-    pad_ref[radius + frames :] = hi_ref[...]
-    taps = [
-        jnp.full((SUB, LANES), k_ref[count - 1 - a if flip else a], jnp.float32)
-        for a in range(count)
-    ]
-    rows_of = scans // SUB
+        total = None
+        for a, tap in enumerate(taps):
+            part = tap * src[frame, pl.ds(SUB - radius + a, scans), :]
+            total = part if total is None else total + part
+        emit(frame, total)
+        return carry
+
+    lax.fori_loop(0, src.shape[0], one, 0, unroll=4)
+
+
+def blur_frames(scalars, src, frames, emit):
+    count = len(scalars)
+    taps = [jnp.full((SUB, LANES), tap, jnp.float32) for tap in scalars]
+    rows_of = src.shape[1] // SUB
 
     def block(index, carry):
         first = (index // rows_of) * STEP
-        rows = pl.ds(pl.multiple_of((index % rows_of) * SUB, SUB), SUB)
+        start = lax.rem(index, rows_of) * SUB
+        rows = pl.ds(pl.multiple_of(start, SUB), SUB)
         totals = [None] * STEP
         for j in range(STEP + count - 1):
-            value = pad_ref[first + j, rows, :]
+            value = src[first + j, rows, :]
             for i in range(STEP):
                 if 0 <= j - i < count:
                     part = taps[j - i] * value
                     totals[i] = part if totals[i] is None else totals[i] + part
         for i in range(STEP):
-            result = totals[i]
-            if divide:
-                result = above[0][first + i, rows, :] / result
-            out_ref[first + i, rows, :] = result
+            emit(first + i, start, totals[i])
         return carry
 
     lax.fori_loop(0, (frames // STEP) * rows_of, block, 0)
 
 
-def blur(body, taps, arrays, pad_shape):
-    frames, scans, channels = arrays[0].shape
-
-    def spec(array):
-        return pl.BlockSpec((array.shape[0], array.shape[1], LANES), lambda c: (0, 0, c))
-
+def deblur_body(sizes, fk_ref, sk_ref, obs_ref, out_ref, *scratch):
+    est, blurred, ratio, back, send, recv, swap_send, swap_recv, own_sem = scratch
+    rt_size, mob_size = sizes
+    frames, scans, channels = obs_ref.shape
+    half = channels // 2
+    tiles = half // LANES
+    long = 2 * frames
+    radius = (fk_ref.shape[0] - 1) // 2
+    rt, mob = lax.axis_index("rt"), lax.axis_index("mob")
+    side = lax.rem(rt, 2)
+    mid = pl.ds(SUB, scans)
+    has = {
+        ("rt", 0): rt >= 2,
+        ("rt", 1): rt < rt_size - 2,
+        ("mob", 0): mob > 0,
+        ("mob", 1): mob < mob_size - 1,
+    }
+    to = {
+        ("rt", 0): lax.rem(rt + rt_size - 2, rt_size),
+        ("rt", 1): lax.rem(rt + 2, rt_size),
+        ("mob", 0): lax.rem(mob + mob_size - 1, mob_size),
+        ("mob", 1): lax.rem(mob + 1, mob_size),
+    }
+    mate = lax.bitwise_xor(rt, 1)
+    mesh_type = pl.DeviceIdType.MESH
+
+    barrier = pltpu.get_barrier_semaphore()
+    pl.semaphore_signal(barrier, inc=1, device_id={"rt": mate}, device_id_type=mesh_type)
+    for key in has:
+
+        @pl.when(has[key])
+        def _(key=key):
+            pl.semaphore_signal(
+                barrier, inc=1, device_id={key[0]: to[key]}, device_id_type=mesh_type
+            )
+
+    peers = 1
+    for key in has:
+        peers = peers + has[key].astype(jnp.int32)
+    pl.semaphore_wait(barrier, peers)
+
+    def lanes_of(which, c):
+        return pl.ds(pl.multiple_of(which * half + c * LANES, LANES), LANES)
+
+    def landing(c):
+        return est.at[0, c, pl.ds(side * frames, frames), mid, :]
+
+    def swap_in_remote(c):
+        return pltpu.make_async_remote_copy(
+            src_ref=obs_ref.at[:, :, lanes_of(1 - side, c)],
+            dst_ref=landing(c),
+            send_sem=swap_send.at[0, c],
+            recv_sem=swap_recv.at[0, c],
+            device_id={"rt": mate},
+            device_id_type=mesh_type,
+        )
+
+    def swap_in(c):
+        own = pltpu.make_async_copy(
+            obs_ref.at[:, :, lanes_of(side, c)], landing(c), own_sem.at[0, c]
+        )
+        return swap_in_remote(c), own
+
+    def swap_out(c):
+        away = pltpu.make_async_remote_copy(
+            src_ref=est.at[ITERS, c, pl.ds((1 - side) * frames, frames), mid, :],
+            dst_ref=out_ref.at[:, :, lanes_of(side, c)],
+            send_sem=swap_send.at[1, c],
+            recv_sem=swap_recv.at[1, c],
+            device_id={"rt": mate},
+            device_id_type=mesh_type,
+        )
+        own = pltpu.make_async_copy(
+            est.at[ITERS, c, pl.ds(side * frames, frames), mid, :],
+            out_ref.at[:, :, lanes_of(side, c)],
+            own_sem.at[1, c],
+        )
+        return away, own
+
+    def start_both(pair):
+        pair[0].start()
+        pair[1].start()
+
+    fields = (est, blurred, ratio, back)
+
+    def halo(kind, it, c, way):
+        cells = fields[kind].at[it, c]
+        if kind in (0, 3):
+            axis = "mob"
+            src = cells.at[:, pl.ds(scans if way else SUB, SUB), :]
+            dst = cells.at[:, pl.ds(0 if way else SUB + scans, SUB), :]
+        else:
+            axis = "rt"
+            src = cells.at[pl.ds(long if way else radius, radius)]
+            dst = cells.at[pl.ds(0 if way else radius + long, radius)]
+        return axis, pltpu.make_async_remote_copy(
+            src_ref=src,
+            dst_ref=dst,
+            send_sem=send.at[kind, it, c, way],
+            recv_sem=recv.at[kind, it, c, way],
+            device_id={axis: to[axis, way]},
+            device_id_type=mesh_type,
+        )
+
+    def on_halo(kind, it, c, act, flip):
+        axis = "mob" if kind in (0, 3) else "rt"
+        for way in (0, 1):
+
+            @pl.when(has[axis, 1 - way if flip else way])
+            def _(way=way):
+                act(halo(kind, it, c, way)[1])
+
+    def start_halo(kind, it, c):
+        on_halo(kind, it, c, lambda copy: copy.start(), False)
+
+    def wait_halo(kind, it, c):
+        on_halo(kind, it, c, lambda copy: copy.wait_recv(), True)
+
+    def begin(c, carry):
+        start_both(swap_in(c))
+        return carry
+
+    lax.fori_loop(0, tiles, begin, 0)
+
+    def clear(index, carry):
+        it, c = index // tiles, lax.rem(index, tiles)
+        for field in (est, back):
+            for way, start in ((0, 0), (1, SUB + scans)):
+
+                @pl.when(jnp.logical_not(has["mob", way]))
+                def _(field=field, start=start):
+                    field[it, c, :, pl.ds(start, SUB), :] = jnp.zeros(
+                        (long, SUB, LANES), jnp.float32
+                    )
+
+        for field in (blurred, ratio):
+            for way, start in ((0, 0), (1, radius + long)):
+
+                @pl.when(jnp.logical_not(has["rt", way]))
+                def _(field=field, start=start):
+                    field[it, c, pl.ds(start, radius)] = jnp.zeros(
+                        (radius, scans, LANES), jnp.float32
+                    )
+
+        return carry
+
+    lax.fori_loop(0, ITERS * tiles, clear, 0)
+
+    def arrive(c):
+        away, own = swap_in(c)
+        own.wait()
+        away.wait_recv()
+        start_halo(0, 0, c)
+
+    def forward_scans(it, c):
+        wait_halo(0, it, c)
+
+        def emit(frame, total):
+            blurred[it, c, radius + frame] = total
+
+        blur_scans(flipped(sk_ref, False), est.at[it, c], scans, emit)
+        start_halo(1, it, c)
+
+    def forward_frames(it, c):
+        wait_halo(1, it, c)
+
+        def emit(frame, start, total):
+            seen = est[0, c, frame, pl.ds(pl.multiple_of(SUB + start, SUB), SUB), :]
+            ratio[it, c, radius + frame, pl.ds(pl.multiple_of(start, SUB), SUB), :] = seen / total
+
+        blur_frames(flipped(fk_ref, False), blurred.at[it, c], long, emit)
+        start_halo(2, it, c)
+
+    def back_frames(it, c):
+        wait_halo(2, it, c)
+
+        def emit(frame, start, total):
+            back[it, c, frame, pl.ds(pl.multiple_of(SUB + start, SUB), SUB), :] = total
+
+        blur_frames(flipped(fk_ref, True), ratio.at[it, c], long, emit)
+        start_halo(3, it, c)
+
+    def back_scans(it, c):
+        wait_halo(3, it, c)
+
+        def emit(frame, total):
+            est[it + 1, c, frame, mid, :] = est[it, c, frame, mid, :] * total
+
+        blur_scans(flipped(sk_ref, True), back.at[it, c], scans, emit)
+
+        @pl.when(it < ITERS - 1)
+        def _():
+            start_halo(0, it + 1, c)
+
+        @pl.when(it == ITERS - 1)
+        def _():
+            start_both(swap_out(c))
+
+    steps = (forward_scans, forward_frames, back_frames, back_scans)
+    total_steps = len(steps) * ITERS
+    arrive(0)
+
+    def wave(t, carry):
+        def tile(c, inner):
+            stage = t - c
+            live = jnp.logical_and(stage >= 0, stage < total_steps)
+            for n, step in enumerate(steps):
+
+                @pl.when(jnp.logical_and(live, lax.rem(stage + total_steps, len(steps)) == n))
+                def _(step=step):
+                    step(stage // len(steps), c)
+
+            return inner
+
+        lax.fori_loop(0, tiles, tile, 0)
+
+        @pl.when(t + 1 < tiles)
+        def _():
+            arrive(t + 1)
+
+        return carry
+
+    lax.fori_loop(0, total_steps + tiles - 1, wave, 0)
+
+    def finish(c, carry):
+        away, own = swap_out(c)
+        own.wait()
+        away.wait()
+        swap_in_remote(c).wait_send()
+        return carry
+
+    lax.fori_loop(0, tiles, finish, 0)
+
+    def sent(index, carry):
+        it, c = index // tiles, lax.rem(index, tiles)
+        for kind in range(len(fields)):
+            on_halo(kind, it, c, lambda copy: copy.wait_send(), False)
+        return carry
+
+    lax.fori_loop(0, ITERS * tiles, sent, 0)
+
+
+def deblur(observed, frame_kernel, scan_kernel):
+    frames, scans, channels = observed.shape
+    tiles = channels // 2 // LANES
+    radius = (frame_kernel.shape[0] - 1) // 2
+    sizes = lax.axis_size("rt"), lax.axis_size("mob")
+    tall = (2 * frames, scans + 2 * SUB, LANES)
+    long = (2 * frames + 2 * radius, scans, LANES)
+    smem = pl.BlockSpec(memory_space=pltpu.SMEM)
+    anywhere = pl.BlockSpec(memory_space=pl.ANY)
+    dma = pltpu.SemaphoreType.DMA
     return pl.pallas_call(
-        body,
-        grid=(channels // LANES,),
-        in_specs=[pl.BlockSpec(memory_space=pltpu.SMEM)] + [spec(a) for a in arrays],
-        out_specs=pl.BlockSpec((frames, scans, LANES), lambda c: (0, 0, c)),
-        out_shape=jax.ShapeDtypeStruct((frames, scans, channels), jnp.float32),
-        scratch_shapes=[pltpu.VMEM(pad_shape, jnp.float32)],
-        compiler_params=pltpu.CompilerParams(vmem_limit_bytes=32 * 1024 * 1024),
+        functools.partial(deblur_body, sizes),
+        in_specs=[smem, smem, anywhere],
+        out_specs=anywhere,
+        out_shape=jax.ShapeDtypeStruct(observed.shape, jnp.float32),
+        scratch_shapes=[
+            pltpu.VMEM((ITERS + 1, tiles) + tall, jnp.float32),
+            pltpu.VMEM((ITERS, tiles) + long, jnp.float32),
+            pltpu.VMEM((ITERS, tiles) + long, jnp.float32),
+            pltpu.VMEM((ITERS, tiles) + tall, jnp.float32),
+            dma((4, ITERS, tiles, 2)),
+            dma((4, ITERS, tiles, 2)),
+            dma((2, tiles)),
+            dma((2, tiles)),
+            dma((2, tiles)),
+        ],
+        compiler_params=pltpu.CompilerParams(
+            collective_id=2, has_side_effects=True, vmem_limit_bytes=50 * 1024 * 1024
+        ),
         cost_estimate=pl.CostEstimate(
-            flops=2 * taps.shape[0] * frames * scans * channels,
-            bytes_accessed=12 * frames * scans * channels,
+            flops=4 * ITERS * (frame_kernel.shape[0] + scan_kernel.shape[0]) * observed.size,
+            bytes_accessed=8 * observed.size,
             transcendentals=0,
         ),
-    )(taps, *arrays)
-
-
-def halo(cells, axis, dim, width, hop):
-    count = lax.axis_size(axis)
-    size = cells.shape[dim]
-    up = [(i, i + hop) for i in range(count - hop)]
-    down = [(i + hop, i) for i in range(count - hop)]
-    before = lax.ppermute(lax.slice_in_dim(cells, size - width, size, axis=dim), axis, up)
-    after = lax.ppermute(lax.slice_in_dim(cells, 0, width, axis=dim), axis, down)
-    return before, after
+    )(frame_kernel, scan_kernel, observed)
 
 
 def partner(axis, bit):
@@ -251,46 +478,7 @@
 
 
 def local(observed, frame_kernel, scan_kernel, prec_window, frag_window):
-    frames, scan_count, channels = observed.shape
-    radius = (frame_kernel.shape[0] - 1) // 2
-    half = channels // 2
-    count = lax.axis_size("rt")
-    side = lax.rem(lax.axis_index("rt"), 2)
-    swap = [(i, i ^ 1) for i in range(count)]
-
-    def blur_scans(flip, cells, *scale):
-        before, after = halo(cells, "mob", 1, SUB, 1)
-        return blur(
-            functools.partial(scan_kernel_body, flip),
-            scan_kernel,
-            (cells, before, after) + scale,
-            (cells.shape[0], scan_count + 2 * SUB, LANES),
-        )
-
-    def blur_frames(flip, cells, *above):
-        before, after = halo(cells, "rt", 0, radius, 2)
-        return blur(
-            functools.partial(frame_kernel_body, flip, bool(above)),
-            frame_kernel,
-            (cells, before, after) + above,
-            (cells.shape[0] + 2 * radius, scan_count, LANES),
-        )
-
-    mine = lax.dynamic_slice_in_dim(observed, side * half, half, axis=2)
-    other = lax.dynamic_slice_in_dim(observed, (1 - side) * half, half, axis=2)
-    other = lax.ppermute(other, "rt", swap)
-    first = side == 0
-    wide = jnp.concatenate([jnp.where(first, mine, other), jnp.where(first, other, mine)], axis=0)
-    estimate = wide
-    for iteration in range(ITERS):
-        ratio = blur_frames(False, blur_scans(False, estimate), wide)
-        estimate = blur_scans(True, blur_frames(True, ratio), estimate)
-    mine = lax.dynamic_slice_in_dim(estimate, side * frames, frames, axis=0)
-    other = lax.dynamic_slice_in_dim(estimate, (1 - side) * frames, frames, axis=0)
-    other = lax.ppermute(other, "rt", swap)
-    estimate = jnp.concatenate(
-        [jnp.where(first, mine, other), jnp.where(first, other, mine)], axis=2
-    )
+    estimate = deblur(observed, frame_kernel, scan_kernel)
     return (estimate, correlate(estimate, prec_window, frag_window))
 
 

time: 306 us -> 149 us (0.49)
  waiting for transfers between devices: 109 us -> 0 us
  starting transfers between devices: 74 us -> 0 us
  Pallas kernels: 107 us -> 144 us
  local copies, waits for them, and re-layouts: 9.92 us -> 4.16 us
  other arithmetic: 3.65 us -> 0 us
    ppermute x18 -> x0, waiting for transfers between devices: 109 us -> none  [the longest x2 45.3 us: local(): other = lax.ppermute(other, 'rt', swap)]
    ppermute x18 -> x0, starting transfers between devices: 74 us -> none  [the longest x8 59.2 us: halo(): lax.ppermute(lax.slice_in_dim(cells, size - width, size, axis=dim), axis,...]
    pallas_call x8 -> x1, Pallas kernels: 52 us -> 99.7 us  [deblur(): pl.pallas_call(functools.partial(deblur_body, sizes), in_specs=[smem, sme...]
    pallas_call x1, Pallas kernels: 54.9 us -> 44.6 us  [correlate(): pl.pallas_call(functools.partial(correlate_body, stages, (mobs, rows_of),...]
  transfers between devices with their start and end apart: 18 -> 0, of which waited for: 18 -> 0; matrix products, arithmetic and copies ran while one was open for 0% -> 0% of each run, Pallas kernels for 0% -> 0%
where the time goes in v3:
time: 149 us
  Pallas kernels  144 us (97%)
  local copies, waits for them, and re-layouts  4.16 us (3%)
    pallas_call x1, Pallas kernels, deblur(): pl.pallas_call(functools.partial(deblur_body, sizes), in_specs=[smem, sme...  99.7 us
    pallas_call x1, Pallas kernels, correlate(): pl.pallas_call(functools.partial(correlate_body, stages, (mobs, rows_of),...  44.6 us
    unnamed x8, local copies, waits for them, and re-layouts  3.42 us

profile of v3, /device:TPU:0, one launch (start us, length us, event | category | flops | bytes accessed | tf_op | source)
XLA Modules:
  0.0 149.1 jit_solution(5118845172727674475)
XLA Ops:
  0.6 0.7 copy.7.prow_ref
  1.4 0.0 copy-start.1
  1.4 0.7 copy-done.1
  2.0 0.0 copy-start.2
  2.0 0.7 copy-done.2
  2.7 0.0 copy-start
  2.7 99.7 %shard_map.68 = f32[32,16,1280]{2,1,0:T(8,128)S(1)} custom-call(f32[31]{0:T(128)S(1)} %copy-done.1, f32[15]{0:T(128)S(1)} %copy-done.2, f32[32,16,1280]{2,1,0:T(8,128)} %obs_ref.1), custom_call_target="tpu_custom_call" | custom-call | flops 241172480 | bytes 5242880 | tf_op jit(solution)/shard_map/pallas_call | solution.py:311
  102.3 0.0 copy-done
  102.4 44.6 %shard_map.69 = f32[32,256]{1,0:T(8,128)S(1)} custom-call(f32[512,1280]{1,0:T(8,128)S(1)} %bitcast.3, s32[32,1]{1,0:T(8,128)S(1)} %copy.7.prow_ref, s32[1,256]{1,0:T(1,128)S(1)} %bitcast.4), custom_call_target="tpu_custom_call" | custom-call | flops 268435456 | bytes 2621440 | tf_op jit(solution)/shard_map/pallas_call | solution.py:450
  147.0 1.5 %copy.10 = f32[32,16,1280]{2,1,0:T(8,128)} copy(f32[32,16,1280]{2,1,0:T(8,128)S(1)} %shard_map.68) | data formatting | bytes 5242880
  148.5 0.6 copy.11
Async XLA Ops:
  1.4 0.7 copy-start.1
  2.0 0.7 copy-start.2
  2.7 99.7 %copy-start = (s32[256]{0:T(256)S(1)}, s32[256]{0:T(256)}, u32[]{:S(2)}) copy-start(s32[256]{0:T(256)} %param.9) | copy-start | bytes 3076

commit v4 on v3

--- a/solution.py
+++ b/solution.py
@@ -12,6 +12,8 @@
 LANES = 128
 SUB = 8
 STEP = 16
+AHEAD = 2
+CHUNKS = 2
 
 
 def flipped(k_ref, flip):
@@ -178,7 +180,7 @@
         start_both(swap_in(c))
         return carry
 
-    lax.fori_loop(0, tiles, begin, 0)
+    lax.fori_loop(0, min(AHEAD, tiles), begin, 0)
 
     def clear(index, carry):
         it, c = index // tiles, lax.rem(index, tiles)
@@ -208,6 +210,11 @@
         away, own = swap_in(c)
         own.wait()
         away.wait_recv()
+
+        @pl.when(c + AHEAD < tiles)
+        def _():
+            start_both(swap_in(c + AHEAD))
+
         start_halo(0, 0, c)
 
     def forward_scans(it, c):
@@ -377,20 +384,24 @@
     mobs, rows_of = groups
     prec = est_ref.shape[1] - mobs * out_ref.shape[1]
     rows, columns = out_ref.shape
+    part = columns // CHUNKS
     greet(stages)
-    sums[0] = jnp.broadcast_to(
-        jnp.sum(est_ref[...], axis=0, keepdims=True), sums.shape[1:]
-    )
+    here = jnp.sum(est_ref[...], axis=0, keepdims=True)
+    lane_tiles = est_ref.shape[1] // LANES
+    sums[0] = jnp.zeros(sums.shape[1:], jnp.float32)
+    for k in range(lane_tiles):
+        sums[0, k : k + 1, :] = here[:, k * LANES : (k + 1) * LANES]
     for n, stage in enumerate(stages):
         copy = exchange(sums.at[n], got.at[n], sum_send.at[n], sum_recv.at[n], stage)
         copy.wait()
         sums[n + 1] = sums[n] + got[n]
-    mean = sums[count, :1, :] / cells
+    mean = jnp.concatenate([sums[count, k : k + 1, :] for k in range(lane_tiles)], axis=1) / cells
     left = (est_ref[:, :prec] - mean[:, :prec]).astype(jnp.bfloat16)
     wide = left.astype(jnp.float32)
     left_squares = jnp.sum(wide * wide, axis=0, keepdims=True)
     across = left.T
     first = held[0]
+    upper = lax.broadcasted_iota(jnp.int32, (SUB, columns), 0) < SUB // 2
     for m in range(mobs):
         start = prec + m * columns
         right = (
@@ -398,36 +409,50 @@
         ).astype(jnp.bfloat16)
         wide = right.astype(jnp.float32)
         right_squares = jnp.sum(wide * wide, axis=0, keepdims=True)
+        squares = jnp.where(upper, right_squares, left_squares)
         product = jnp.dot(across, right, preferred_element_type=jnp.float32)
         for r in range(rows_of):
-            block = first.at[m // 2, m % 2, r]
-            block[:rows, :] = product[r * rows : (r + 1) * rows, :]
-            block[rows : rows + 8, :] = jnp.broadcast_to(right_squares, (8, columns))
-            block[rows + 8 :, :] = jnp.broadcast_to(left_squares, (8, prec))
-    for n, stage in enumerate(stages):
-        axis, bit = stage
+            for k in range(CHUNKS):
+                block = first.at[k, m // 2, m % 2, r]
+                block[:rows, :] = product[r * rows : (r + 1) * rows, k * part : (k + 1) * part]
+                block[rows:, :] = squares[:, k * part : (k + 1) * part]
+
+    def send_chunk(n, k):
+        axis, bit = stages[n]
         mine = lax.rem(lax.axis_index(axis) // bit, 2)
-        copy = exchange(
-            held[n].at[:, 1 - mine], landed[n], send_sem.at[n], recv_sem.at[n], stage
-        )
-        copy.wait()
-        span = held[n].shape[0]
-        for i in range(span):
-            total = held[n][i, mine] + landed[n][i]
-            if n + 1 == count:
-                column = 1.0 / jnp.sqrt(total[rows : rows + 1, :] + 1e-06)
-                row = 1.0 / jnp.sqrt(total[rows + 8 : rows + 9, :] + 1e-06)
-                place = lax.broadcasted_iota(jnp.int32, (rows, prec), 1)
-                wanted = lax.broadcasted_iota(jnp.int32, (rows, prec), 0)
-                wanted = wanted + lax.axis_index("rt") * rows
-                row = jnp.sum(jnp.where(place == wanted, row, 0.0), axis=1, keepdims=True)
-                same = (prow_ref[...] == fcol_ref[...]).astype(jnp.float32)
-                out_ref[...] = same * total[:rows, :] * row * column
-            elif stages[n + 1][0] == axis:
-                held[n + 1][i // 2, i % 2] = total
-            else:
-                for r in range(rows_of):
-                    held[n + 1][r // 2, r % 2] = total[r]
+        return exchange(
+            held[n].at[k, :, 1 - mine],
+            landed[n].at[k],
+            send_sem.at[n, k],
+            recv_sem.at[n, k],
+            stages[n],
+        )
+
+    copies = [send_chunk(0, k) for k in range(CHUNKS)]
+    totals = [None] * CHUNKS
+    for n, (axis, bit) in enumerate(stages):
+        mine = lax.rem(lax.axis_index(axis) // bit, 2)
+        for k in range(CHUNKS):
+            copies[k].wait()
+            for i in range(held[n].shape[1]):
+                total = held[n][k, i, mine] + landed[n][k, i]
+                if n + 1 == count:
+                    totals[k] = total
+                elif stages[n + 1][0] == axis:
+                    held[n + 1][k, i // 2, i % 2] = total
+                else:
+                    for r in range(rows_of):
+                        held[n + 1][k, r // 2, r % 2] = total[r]
+            if n + 1 < count:
+                copies[k] = send_chunk(n + 1, k)
+    total = jnp.concatenate(totals, axis=1)
+    column = 1.0 / jnp.sqrt(total[rows : rows + 1, :] + 1e-06)
+    row = 1.0 / jnp.sqrt(total[rows + SUB // 2 : rows + SUB // 2 + 1, :] + 1e-06)
+    place = lax.broadcasted_iota(jnp.int32, (rows, prec), 1)
+    wanted = lax.broadcasted_iota(jnp.int32, (rows, prec), 0) + lax.axis_index("rt") * rows
+    row = jnp.sum(jnp.where(place == wanted, row, 0.0), axis=1, keepdims=True)
+    same = (prow_ref[...] == fcol_ref[...]).astype(jnp.float32)
+    out_ref[...] = same * total[:rows, :] * row * column
 
 
 def correlate(estimate, prec_window, frag_window):
@@ -436,15 +461,16 @@
     rows, columns = prec_window.shape[0], frag_window.shape[0]
     stages = [("mob", bit) for bit in bits_of(mobs)] + [("rt", bit) for bit in bits_of(rows_of)]
     count = len(stages)
-    tile = (rows + 16, columns)
+    tile = (rows + SUB, columns // CHUNKS)
+    sum_rows = -(-channels // (LANES * SUB)) * SUB
     held, landed = [], []
     for axis, bit in stages:
         if axis == "mob":
             span, tail = mobs // (2 * bit), (rows_of,) + tile
         else:
             span, tail = rows_of // (2 * bit), tile
-        held.append(pltpu.VMEM((span, 2) + tail, jnp.float32))
-        landed.append(pltpu.VMEM((span,) + tail, jnp.float32))
+        held.append(pltpu.VMEM((CHUNKS, span, 2) + tail, jnp.float32))
+        landed.append(pltpu.VMEM((CHUNKS, span) + tail, jnp.float32))
     whole = pl.BlockSpec(memory_space=pltpu.VMEM)
     cells = frames * scans * mobs * rows_of
     return pl.pallas_call(
@@ -453,12 +479,12 @@
         out_specs=whole,
         out_shape=jax.ShapeDtypeStruct((rows, columns), jnp.float32),
         scratch_shapes=[
-            pltpu.VMEM((count + 1, SUB, channels), jnp.float32),
-            pltpu.VMEM((count, SUB, channels), jnp.float32),
+            pltpu.VMEM((count + 1, sum_rows, LANES), jnp.float32),
+            pltpu.VMEM((count, sum_rows, LANES), jnp.float32),
             pltpu.SemaphoreType.DMA((count,)),
             pltpu.SemaphoreType.DMA((count,)),
-            pltpu.SemaphoreType.DMA((count,)),
-            pltpu.SemaphoreType.DMA((count,)),
+            pltpu.SemaphoreType.DMA((count, CHUNKS)),
+            pltpu.SemaphoreType.DMA((count, CHUNKS)),
         ]
         + held
         + landed,

time: 149 us -> 142 us (0.953)
  Pallas kernels: 144 us -> 137 us
    pallas_call x1, Pallas kernels: 44.6 us -> 37.1 us  [correlate(): pl.pallas_call(functools.partial(correlate_body, stages, (mobs, rows_of),...]
where the time goes in v4:
time: 142 us
  Pallas kernels  137 us (96%)
  local copies, waits for them, and re-layouts  4.16 us (3%)
    pallas_call x1, Pallas kernels, deblur(): pl.pallas_call(functools.partial(deblur_body, sizes), in_specs=[smem, sme...  99.7 us
    pallas_call x1, Pallas kernels, correlate(): pl.pallas_call(functools.partial(correlate_body, stages, (mobs, rows_of),...  37.1 us
    unnamed x8, local copies, waits for them, and re-layouts  3.42 us

profile of v4, /device:TPU:0, one launch (start us, length us, event | category | flops | bytes accessed | tf_op | source)
XLA Modules:
  0.0 141.6 jit_solution(17426771690837880632)
XLA Ops:
  0.6 0.7 copy.7.prow_ref
  1.4 0.0 copy-start.1
  1.4 0.7 copy-done.1
  2.0 0.0 copy-start.2
  2.0 0.7 copy-done.2
  2.7 0.0 copy-start
  2.7 99.7 %shard_map.68 = f32[32,16,1280]{2,1,0:T(8,128)S(1)} custom-call(f32[31]{0:T(128)S(1)} %copy-done.1, f32[15]{0:T(128)S(1)} %copy-done.2, f32[32,16,1280]{2,1,0:T(8,128)} %obs_ref.1), custom_call_target="tpu_custom_call" | custom-call | flops 241172480 | bytes 5242880 | tf_op jit(solution)/shard_map/pallas_call | solution.py:318
  102.4 0.0 copy-done
  102.4 37.1 %shard_map.69 = f32[32,256]{1,0:T(8,128)S(1)} custom-call(f32[512,1280]{1,0:T(8,128)S(1)} %bitcast.3, s32[32,1]{1,0:T(8,128)S(1)} %copy.7.prow_ref, s32[1,256]{1,0:T(1,128)S(1)} %bitcast.4), custom_call_target="tpu_custom_call" | custom-call | flops 268435456 | bytes 2621440 | tf_op jit(solution)/shard_map/pallas_call | solution.py:476
  139.5 1.5 %copy.10 = f32[32,16,1280]{2,1,0:T(8,128)} copy(f32[32,16,1280]{2,1,0:T(8,128)S(1)} %shard_map.68) | data formatting | bytes 5242880
  141.0 0.6 copy.11
Async XLA Ops:
  1.4 0.7 copy-start.1
  2.0 0.7 copy-start.2
  2.7 99.7 %copy-start = (s32[256]{0:T(256)S(1)}, s32[256]{0:T(256)}, u32[]{:S(2)}) copy-start(s32[256]{0:T(256)} %param.9) | copy-start | bytes 3076

commit v5 on v4

--- a/solution.py
+++ b/solution.py
@@ -385,17 +385,25 @@
     prec = est_ref.shape[1] - mobs * out_ref.shape[1]
     rows, columns = out_ref.shape
     part = columns // CHUNKS
-    greet(stages)
+    peers = [("mob", n) for n in range(1, mobs)] + [("rt", n) for n in range(1, rows_of)]
+    greet(peers)
     here = jnp.sum(est_ref[...], axis=0, keepdims=True)
     lane_tiles = est_ref.shape[1] // LANES
     sums[0] = jnp.zeros(sums.shape[1:], jnp.float32)
     for k in range(lane_tiles):
         sums[0, k : k + 1, :] = here[:, k * LANES : (k + 1) * LANES]
-    for n, stage in enumerate(stages):
-        copy = exchange(sums.at[n], got.at[n], sum_send.at[n], sum_recv.at[n], stage)
-        copy.wait()
-        sums[n + 1] = sums[n] + got[n]
-    mean = jnp.concatenate([sums[count, k : k + 1, :] for k in range(lane_tiles)], axis=1) / cells
+    for n, axis in enumerate(("mob", "rt")):
+        slots = [i for i, peer in enumerate(peers) if peer[0] == axis]
+        flying = [
+            exchange(sums.at[n], got.at[i], sum_send.at[i], sum_recv.at[i], peers[i])
+            for i in slots
+        ]
+        total = sums[n]
+        for i, copy in zip(slots, flying):
+            copy.wait()
+            total = total + got[i]
+        sums[n + 1] = total
+    mean = jnp.concatenate([sums[2, k : k + 1, :] for k in range(lane_tiles)], axis=1) / cells
     left = (est_ref[:, :prec] - mean[:, :prec]).astype(jnp.bfloat16)
     wide = left.astype(jnp.float32)
     left_squares = jnp.sum(wide * wide, axis=0, keepdims=True)
@@ -461,6 +469,7 @@
     rows, columns = prec_window.shape[0], frag_window.shape[0]
     stages = [("mob", bit) for bit in bits_of(mobs)] + [("rt", bit) for bit in bits_of(rows_of)]
     count = len(stages)
+    peers = mobs + rows_of - 2
     tile = (rows + SUB, columns // CHUNKS)
     sum_rows = -(-channels // (LANES * SUB)) * SUB
     held, landed = [], []
@@ -479,10 +488,10 @@
         out_specs=whole,
         out_shape=jax.ShapeDtypeStruct((rows, columns), jnp.float32),
         scratch_shapes=[
-            pltpu.VMEM((count + 1, sum_rows, LANES), jnp.float32),
-            pltpu.VMEM((count, sum_rows, LANES), jnp.float32),
-            pltpu.SemaphoreType.DMA((count,)),
-            pltpu.SemaphoreType.DMA((count,)),
+            pltpu.VMEM((3, sum_rows, LANES), jnp.float32),
+            pltpu.VMEM((peers, sum_rows, LANES), jnp.float32),
+            pltpu.SemaphoreType.DMA((peers,)),
+            pltpu.SemaphoreType.DMA((peers,)),
             pltpu.SemaphoreType.DMA((count, CHUNKS)),
             pltpu.SemaphoreType.DMA((count, CHUNKS)),
         ]

time: 142 us -> 137 us (0.965)
  Pallas kernels: 137 us -> 132 us
    pallas_call x1, Pallas kernels: 37.1 us -> 32.5 us  [correlate(): pl.pallas_call(functools.partial(correlate_body, stages, (mobs, rows_of),...]
where the time goes in v5:
time: 137 us
  Pallas kernels  132 us (96%)
  local copies, waits for them, and re-layouts  4.16 us (3%)
    pallas_call x1, Pallas kernels, deblur(): pl.pallas_call(functools.partial(deblur_body, sizes), in_specs=[smem, sme...  99.7 us
    pallas_call x1, Pallas kernels, correlate(): pl.pallas_call(functools.partial(correlate_body, stages, (mobs, rows_of),...  32.5 us
    unnamed x8, local copies, waits for them, and re-layouts  3.42 us

profile of v5, /device:TPU:0, one launch (start us, length us, event | category | flops | bytes accessed | tf_op | source)
XLA Modules:
  0.0 137.0 jit_solution(7984861168595518929)
XLA Ops:
  0.6 0.7 copy.7.prow_ref
  1.4 0.0 copy-start.1
  1.4 0.7 copy-done.1
  2.0 0.0 copy-start.2
  2.0 0.7 copy-done.2
  2.7 0.0 copy-start
  2.7 99.7 %shard_map.68 = f32[32,16,1280]{2,1,0:T(8,128)S(1)} custom-call(f32[31]{0:T(128)S(1)} %copy-done.1, f32[15]{0:T(128)S(1)} %copy-done.2, f32[32,16,1280]{2,1,0:T(8,128)} %obs_ref.1), custom_call_target="tpu_custom_call" | custom-call | flops 241172480 | bytes 5242880 | tf_op jit(solution)/shard_map/pallas_call | solution.py:318
  102.4 0.0 copy-done
  102.4 32.5 %shard_map.69 = f32[32,256]{1,0:T(8,128)S(1)} custom-call(f32[512,1280]{1,0:T(8,128)S(1)} %bitcast.3, s32[32,1]{1,0:T(8,128)S(1)} %copy.7.prow_ref, s32[1,256]{1,0:T(1,128)S(1)} %bitcast.4), custom_call_target="tpu_custom_call" | custom-call | flops 268435456 | bytes 2621440 | tf_op jit(solution)/shard_map/pallas_call | solution.py:485
  134.9 1.5 %copy.10 = f32[32,16,1280]{2,1,0:T(8,128)} copy(f32[32,16,1280]{2,1,0:T(8,128)S(1)} %shard_map.68) | data formatting | bytes 5242880
  136.4 0.6 copy.11
Async XLA Ops:
  1.4 0.7 copy-start.1
  2.0 0.7 copy-start.2
  2.7 99.7 %copy-start = (s32[256]{0:T(256)S(1)}, s32[256]{0:T(256)}, u32[]{:S(2)}) copy-start(s32[256]{0:T(256)} %param.9) | copy-start | bytes 3076

commit v6 on v5

--- a/solution.py
+++ b/solution.py
@@ -32,7 +32,7 @@
         emit(frame, total)
         return carry
 
-    lax.fori_loop(0, src.shape[0], one, 0, unroll=4)
+    lax.fori_loop(0, src.shape[0], one, 0, unroll=8)
 
 
 def blur_frames(scalars, src, frames, emit):

time: 137 us -> 136 us (level)
  no operation moved by 1% of the time
where the time goes in v6:
time: 136 us
  Pallas kernels  131 us (96%)
  local copies, waits for them, and re-layouts  4.16 us (3%)
    pallas_call x1, Pallas kernels, deblur(): pl.pallas_call(functools.partial(deblur_body, sizes), in_specs=[smem, sme...  98.8 us
    pallas_call x1, Pallas kernels, correlate(): pl.pallas_call(functools.partial(correlate_body, stages, (mobs, rows_of),...  32.7 us
    unnamed x8, local copies, waits for them, and re-layouts  3.42 us

profile of v6, /device:TPU:0, one launch (start us, length us, event | category | flops | bytes accessed | tf_op | source)
XLA Modules:
  0.0 136.3 jit_solution(553263531764373192)
XLA Ops:
  0.6 0.7 copy.7.prow_ref
  1.4 0.0 copy-start.1
  1.4 0.7 copy-done.1
  2.0 0.0 copy-start.2
  2.0 0.7 copy-done.2
  2.7 0.0 copy-start
  2.7 98.8 %shard_map.68 = f32[32,16,1280]{2,1,0:T(8,128)S(1)} custom-call(f32[31]{0:T(128)S(1)} %copy-done.1, f32[15]{0:T(128)S(1)} %copy-done.2, f32[32,16,1280]{2,1,0:T(8,128)} %obs_ref.1), custom_call_target="tpu_custom_call" | custom-call | flops 241172480 | bytes 5242880 | tf_op jit(solution)/shard_map/pallas_call | solution.py:318
  101.5 0.0 copy-done
  101.5 32.7 %shard_map.69 = f32[32,256]{1,0:T(8,128)S(1)} custom-call(f32[512,1280]{1,0:T(8,128)S(1)} %bitcast.3, s32[32,1]{1,0:T(8,128)S(1)} %copy.7.prow_ref, s32[1,256]{1,0:T(1,128)S(1)} %bitcast.4), custom_call_target="tpu_custom_call" | custom-call | flops 268435456 | bytes 2621440 | tf_op jit(solution)/shard_map/pallas_call | solution.py:485
  134.1 1.5 %copy.10 = f32[32,16,1280]{2,1,0:T(8,128)} copy(f32[32,16,1280]{2,1,0:T(8,128)S(1)} %shard_map.68) | data formatting | bytes 5242880
  135.6 0.6 copy.11
Async XLA Ops:
  1.4 0.7 copy-start.1
  2.0 0.7 copy-start.2
  2.7 98.8 %copy-start = (s32[256]{0:T(256)S(1)}, s32[256]{0:T(256)}, u32[]{:S(2)}) copy-start(s32[256]{0:T(256)} %param.9) | copy-start | bytes 3076
